TPU v7x, 512 devices: a whole 4x8x8 slice. The times are simulated.
512 devices in a mesh: dom: 32 (over x, z_hi, core), orient: 16 (over y, z_lo).
Axes of the slice: x: 4, y: 8, z: 8 (z_hi: 4, z_lo: 2; z = z_hi * 2 + z_lo), core: 2. Of those that a mesh axis runs over, the one named last changes fastest.
Arguments:
- images: bfloat16 [512, 2, 8192], P('dom')
- slices: bfloat16 [1024, 2, 8192], P(('orient', 'dom'))
- noise_weight: float32 [8192], replicated, may hold values from 0.2 to 5
- shifts: int32 [49, 2], replicated, may hold values from -3 to 3, as said below
- kernels: bfloat16 [64, 128, 128], replicated, may hold values from -0.5 to 0.5
- targets: int32 [1024, 64], P('orient'), may hold values from 0 to 1535
Outputs:
- volume: float32 [1536, 2, 128], P(('dom', 'orient'))
- loglik: float32 [512], P('dom')
Inputs may be any that keep to these rules, and one draw needn't show every extreme that they name: `shifts`: translation 0 is the zero shift.
All inputs are finite; a program needn't handle non-finite values.
Results may differ from a plain program's by a relative error of at most 0.0059.
Values may be sent and summed in bfloat16 or wider, within the bound.
A program may use at most 64 MiB of HBM per device.

v0:
```python
import jax
import jax.numpy as jnp
from jax import lax
from jax.sharding import PartitionSpec as P

PIX = 8192
TRANS = 49
BLOCK_PIX = 128
BLOCK_VOX = 128
BLK_DEV = 3
PIX_BLOCKS = 64


def phase_table(shift_rows):
    comp = jnp.arange(PIX, dtype=jnp.int32)
    freq_x = (comp % 64).astype(jnp.float32)
    freq_y = (comp // 64 - PIX // 128).astype(jnp.float32)
    moved = shift_rows.astype(jnp.float32)
    angle = (
        2.0 * jnp.pi * (moved[:, 0:1] * freq_x[None, :] + moved[:, 1:2] * freq_y[None, :]) / 128.0
    )
    return (jnp.cos(angle), jnp.sin(angle))


def align_images(images, shift_rows, noise_weight):
    cosine, sine = phase_table(shift_rows)
    real_part = images[:, 0, :].astype(jnp.float32)[:, None, :]
    imag_part = images[:, 1, :].astype(jnp.float32)[:, None, :]
    out_real = noise_weight * (real_part * cosine - imag_part * sine)
    out_imag = noise_weight * (real_part * sine + imag_part * cosine)
    return jnp.stack([out_real, out_imag], axis=2).astype(jnp.bfloat16)


def shards(images, slices, noise_weight, shifts, kernels, targets):
    group_size = 7
    group_count = TRANS // group_size
    img_rows = images.shape[0]
    ori_rows = slices.shape[0] * lax.axis_size("dom")

    def group_aligned(index):
        rows = lax.dynamic_slice_in_dim(shifts, index * group_size, group_size, 0)
        return align_images(images, rows, noise_weight).reshape(img_rows * group_size, 2 * PIX)

    piece = lax.all_gather(slices, "dom", axis=0, tiled=True)
    count = piece.shape[0]
    energy = 0.5 * jnp.sum(noise_weight * jnp.square(piece.astype(jnp.float32)), axis=(1, 2))
    flat_piece = piece.reshape(count, 2 * PIX)

    def one_group(index):
        aligned = group_aligned(index)
        product = lax.dot_general(
            aligned, flat_piece, (((1,), (1,)), ((), ())), preferred_element_type=jnp.float32
        )
        return product.reshape(img_rows, group_size, count)

    blocks = lax.map(one_group, jnp.arange(group_count, dtype=jnp.int32))
    blocks = jnp.transpose(blocks, (1, 0, 2, 3)).reshape(img_rows, TRANS, count)
    scores = blocks - energy[None, None, :]
    local_peak = jnp.max(scores, axis=(1, 2))
    peak = lax.pmax(local_peak, "orient")
    expo = jnp.exp(scores - peak[:, None, None])
    mass = lax.psum(jnp.sum(expo, axis=(1, 2)), "orient")
    loglik = peak + jnp.log(mass)
    posterior = (expo / mass[:, None, None]).astype(jnp.bfloat16)

    def back_group(index, accum):
        aligned = group_aligned(index)
        weights = lax.dynamic_slice_in_dim(posterior, index * group_size, group_size, 1)
        weights = weights.reshape(img_rows * group_size, ori_rows)
        return accum + lax.dot_general(
            weights, aligned, (((0,), (0,)), ((), ())), preferred_element_type=jnp.float32
        )

    accum = lax.fori_loop(0, group_count, back_group, jnp.zeros((ori_rows, 2 * PIX), jnp.float32))
    blocked = accum.reshape(ori_rows, 2, PIX_BLOCKS, BLOCK_PIX)
    inserted = jnp.einsum(
        "ocbp,bpq->obcq", blocked, kernels.astype(jnp.float32), precision=lax.Precision.HIGHEST
    )
    inserted = inserted.reshape(ori_rows * PIX_BLOCKS, 2 * BLOCK_VOX)
    total_blocks = BLK_DEV * lax.axis_size("dom") * lax.axis_size("orient")
    partial_value = jax.ops.segment_sum(inserted, targets.reshape(-1), num_segments=total_blocks)
    partial_value = partial_value.reshape(total_blocks, 2, BLOCK_VOX)
    volume = lax.psum_scatter(partial_value, ("dom", "orient"), scatter_dimension=0, tiled=True)
    return (volume, loglik)


def solution(mesh):
    placed = (
        P("dom", None, None),
        P(("orient", "dom"), None, None),
        P(),
        P(),
        P(),
        P("orient", None),
    )
    return jax.shard_map(
        shards,
        mesh=mesh,
        in_specs=placed,
        out_specs=(P(("dom", "orient"), None, None), P("dom")),
        check_vma=False,
    )
```

profile of v0, /device:TPU:1, one launch (start us, length us, event | category | flops | bytes accessed | tf_op | source)
XLA Modules:
  0.0 633.6 jit_solution(12740499524834378753)
XLA Ops:
  8.0 1.3 copy.38
  10.2 67.2 %all-gather.2.cloned.1.call-done = bf16[64,2,8192]{2,1,0:T(2,128)(2,1)} async-done(((bf16[2,2,8192]{2,1,0:T(2,128)(2,1)}), bf16[64,2,8192]{2,1,0:T(2,128)(2,1)}) %all-gather.2.cloned.1.call-update) | async-done | bytes 2097168 | tf_op jit(solution)/shard_map/all_gather | solution.py:44
  77.4 4.1 copy.47
  81.5 45.4 %while.28 = (s32[]{:T(128)}, f32[7,16,7,64]{3,1,2,0:T(8,128)S(1)}, f32[8192]{0:T(1024)S(1)}, bf16[16,2,8192]{2,0,1:T(8,128)(2,1)S(1)}, s32[7]{0:T(128)S(1)}, /*i...) while((s32[]{:T(128)}, f32[7,16,7,64]{3,1,2,0:T(8,128)S(1)}, ...), condition=%wide.region_1.2_spmd, body=%wide.region_0.0_spmd.sunk | while | flops 246505488 | bytes 36266464 | solution.py:56
  83.8 1.1 multiply_convert_fusion.6
  85.7 1.2 copy-done.1
  86.9 1.1 fusion.59
  90.3 1.1 multiply_convert_fusion.6
  92.2 1.2 copy-done.1
  93.4 1.1 fusion.59
  96.8 1.1 multiply_convert_fusion.6
  98.7 1.2 copy-done.1
  99.9 1.1 fusion.59
  103.3 1.1 multiply_convert_fusion.6
  105.2 1.2 copy-done.1
  106.3 1.1 fusion.59
  109.8 1.1 multiply_convert_fusion.6
  111.6 1.2 copy-done.1
  112.8 1.1 fusion.59
  116.3 1.1 multiply_convert_fusion.6
  118.1 1.2 copy-done.1
  119.3 1.1 fusion.59
  122.8 1.1 multiply_convert_fusion.6
  124.6 1.2 copy-done.1
  125.8 1.1 fusion.59
  126.9 4.8 multiply_reduce_fusion
  131.9 25.6 %pmax.7 = f32[16]{0:T(128)S(1)} all-reduce(f32[16]{0:T(128)S(1)} %fusion.42), channel_id=1, replica_groups=mesh['dom'=32,'orient'=16] {'orient'}, use_global_device_ids=true, to_apply=%region_4.5 | all-reduce | flops 16 | bytes 128 | tf_op jit(solution)/shard_map/pmax | solution.py:60
  157.7 23.8 %psum.7 = f32[16]{0:T(128)S(1)} all-reduce(f32[16]{0:T(128)S(1)} %exponential_reduce_fusion), channel_id=1, replica_groups=mesh['dom'=32,'orient'=16] {'orient'}, use_global_device_ids=true, to_apply=%region_6.7 | all-reduce | flops 16 | bytes 128 | tf_op jit(solution)/shard_map/psum | solution.py:62
  181.7 114.7 %while.29 = (s32[]{:T(128)}, f32[64,16384]{1,0:T(8,128)}, bf16[16,49,64]{2,0,1:T(8,128)(2,1)S(1)}, f32[8192]{0:T(1024)S(1)}, bf16[16,2,8192]{2,0,1:T(8,128)(2,1)...) while((s32[]{:T(128)}, f32[64,16384]{1,0:T(8,128)}, ...), condition=%wide.region_8.9_spmd.clone, body=%wide.region_7.8_spmd.clone.sunk | while | flops 248602640 | bytes 41552316 | solution.py:74
  182.9 1.1 multiply_convert_fusion.7
  184.4 3.8 copy.64
  188.2 4.0 copy.65
  192.3 4.8 convolution_add_fusion.2
  198.2 1.1 multiply_convert_fusion.7
  199.7 3.8 copy.64
  203.5 4.0 copy.65
  207.6 6.0 convolution_add_fusion.2
  214.8 1.1 multiply_convert_fusion.7
  216.2 3.8 copy.64
  220.0 4.0 copy.65
  224.1 6.0 convolution_add_fusion.2
  231.4 1.1 multiply_convert_fusion.7
  232.8 3.8 copy.64
  236.6 4.0 copy.65
  240.7 6.0 convolution_add_fusion.2
  247.9 1.1 multiply_convert_fusion.7
  249.4 3.8 copy.64
  253.2 4.0 copy.65
  257.3 6.0 convolution_add_fusion.2
  264.5 1.1 multiply_convert_fusion.7
  265.9 3.8 copy.64
  269.7 4.0 copy.65
  273.8 6.0 convolution_add_fusion.2
  281.1 1.1 multiply_convert_fusion.7
  282.5 3.8 copy.64
  286.3 4.0 copy.65
  290.4 6.0 convolution_add_fusion.2
  296.5 2.9 copy.48
  299.4 4.6 fusion.33
  304.0 5.2 copy.42
  309.2 25.2 %scatter_custom_fusion = f32[1536,256]{1,0:T(8,128)} fusion(s32[4096]{0:T(1024)S(1)} %reshape.460, f32[512,8,2,128]{3,2,1,0:T(2,128)} %bitcast.108, f32[]{:T(128)} %constant.191.clone.1), kind=kCustom, calls=%fused_computation.55 | custom fusion | flops 1048576 | bytes 5767172 | tf_op jit(solution)/shard_map/scatter-add | solution.py:81
  334.4 2.9 reshape.453
  337.8 287.6 %all-reduce.3.cloned.1.call-done = f32[1536,2,128]{2,1,0:T(2,128)} async-done(((f32[1536,2,128]{2,1,0:T(2,128)}), f32[1536,2,128]{2,1,0:T(2,128)}) %all-reduce.3.cloned.1.call-update) | async-done | bytes 1572880
  625.5 1.3 constant_dynamic-slice_fusion.1
  (145 shorter events, 31.1 us)
Async XLA Ops:
  7.2 292.2 %copy-start = (bf16[64,128,128]{2,1,0:T(8,128)(2,1)S(1)}, bf16[64,128,128]{2,1,0:T(8,128)(2,1)}, u32[]{:S(2)}) copy-start(bf16[64,128,128]{2,1,0:T(8,128)(2,1)} %param.14) | copy-start | bytes 6291460
  7.2 74.3 %copy-start.2 = (f32[8192]{0:T(1024)S(1)}, f32[8192]{0:T(1024)}, u32[]{:S(2)}) copy-start(f32[8192]{0:T(1024)} %param.12) | copy-start | bytes 98308
  7.2 74.3 %copy-start.3 = (s32[49,2]{0,1:T(2,128)S(1)}, s32[49,2]{0,1:T(2,128)}, u32[]{:S(2)}) copy-start(s32[49,2]{0,1:T(2,128)} %param.13) | copy-start | bytes 1180
  7.2 70.2 %all-gather.2.cloned.1.call-start = ((), (), s32[]{:S(2)}) async-start(), calls=%async_computation | async-start | bytes 2162688 | tf_op jit(solution)/shard_map/all_gather | solution.py:44
  7.9 617.5 %all-reduce.3.cloned.1.call-start = ((), (), s32[]{:S(2)}) async-start(), calls=%async_computation.1 | async-start | bytes 3145728
  85.3 1.6 copy-start.1
  91.8 1.6 copy-start.1
  98.3 1.6 copy-start.1
  104.7 1.6 copy-start.1
  111.2 1.6 copy-start.1
  117.7 1.6 copy-start.1
  124.2 1.6 copy-start.1
Sparse Core Ops, SparseCore 0:
  11.2 66.1 all-gather.1
  337.4 287.9 all-reduce.2
where the time goes:
time: 635 us; the launch traced here: 634 us
  waiting for transfers between devices  356 us (56%)
  local copies, waits for them, and re-layouts  89.1 us (14%)
  other arithmetic  67.1 us (11%)
  matrix products  53.3 us (8%)
  blocking collectives  49.4 us (8%)
  between operations  14.1 us (2%)
    unnamed x3, waiting for transfers between devices  288 us
    all_gather x1, waiting for transfers between devices, shards(): piece = lax.all_gather(slices, 'dom', axis=0, tiled=True)  67.2 us
    dot_general x7, matrix products, back_group(): lax.dot_general(weights, aligned, (((0,), (0,)), ((), ())), preferred_ele...  41.1 us
    while x21, local copies, waits for them, and re-layouts  36.7 us
    another operation x7, local copies, waits for them, and re-layouts, align_images(): return jnp.stack([out_real, out_imag], axis=2).astype(jnp.bfloat16)  26.7 us
    pmax x1, blocking collectives, shards(): peak = lax.pmax(local_peak, 'orient')  25.6 us
    scatter-add x1, other arithmetic, shards(): jax.ops.segment_sum(inserted, targets.reshape(-1), num_segments=total_blo...  25.2 us
    psum x1, blocking collectives, shards(): mass = lax.psum(jnp.sum(expo, axis=(1, 2)), 'orient')  23.8 us
  transfers between devices with their start and end apart: 2, of which 2 were waited for; matrix products, arithmetic and copies ran while one was open for 0% of the time, Pallas kernels for 0%

commit v1 on v0

v1 whole, which is shorter than its diff:
```python
import functools

import jax
import jax.numpy as jnp
import numpy as np
from jax import lax
from jax.experimental import pallas as pl
from jax.experimental.pallas import tpu as pltpu
from jax.sharding import PartitionSpec as P

F32 = jnp.float32
BF16 = jnp.bfloat16
MESH = pl.DeviceIdType.MESH
PIX = 8192
TRANS = 49
FREQ = 64
IMGS = 32
ORI = 32
STEPS = FREQ + 1
VMEM_LIMIT = 56 * 1024 * 1024


def vmem(count):
    return [pl.BlockSpec(memory_space=pltpu.VMEM)] * count


def params(**kw):
    return pltpu.CompilerParams(vmem_limit_bytes=VMEM_LIMIT, **kw)


def tables():
    kx = np.arange(64)
    unit = 2.0 * np.pi / 128.0
    rows = np.zeros((8, 128), np.float32)
    for a in range(4):
        rows[a, :64] = rows[a, 64:] = np.cos(unit * a * kx)
    for a in range(1, 4):
        rows[4 + a, :64] = np.sin(unit * a * kx)
        rows[4 + a, 64:] = -np.sin(unit * a * kx)
    m = np.arange(STEPS)
    sums = np.zeros((STEPS, 8, 128), np.float32)
    for b in range(4):
        sums[:, b, :] = np.cos(unit * b * m)[:, None]
        sums[:, 4 + b, :] = np.where(m == 64, 0.0, np.sin(unit * b * m))[:, None]
    return rows, sums


def fold_kernel(raw_ref, images_ref, slices_ref, rows):
    low = lax.broadcasted_iota(jnp.int32, (18, 128), 1) < 64
    for m in range(FREQ):
        for c in range(2):
            def block(b):
                return raw_ref[:, c * PIX + b * 128 : c * PIX + b * 128 + 128].astype(F32)

            if m % 2 == 0:
                first = block(32 + m // 2)
                second = pltpu.roll(block(32 - m // 2 if m else 0), 64, 1)
            else:
                first = pltpu.roll(block(32 + (m - 1) // 2), 64, 1)
                second = block(32 - (m + 1) // 2)
            both = jnp.where(low, first, second)
            lanes = slice(c * 128, c * 128 + 128)
            images_ref[m, :, lanes] = both[:16].astype(BF16)
            rows[0, m : m + 1, lanes] = both[16:17]
            rows[1, m : m + 1, lanes] = both[17:18]
    slices_ref[...] = rows[...].astype(BF16)


def place():
    dom = lax.axis_index("dom")
    ori = lax.axis_index("orient")
    core = dom % 2
    z_hi = (dom // 2) % 4
    x = dom // 8
    return x, z_hi, core, ori


def gather_kernel(own_images, own_slices, images, slices, send, recv, local):
    x, zh, c, ori = place()

    def dev(xx, zz, cc):
        return (lax.rem(xx + 4, 4) * 8 + lax.rem(zz + 4, 4) * 2 + cc, ori)

    def slot(dx, dz):
        return lax.rem(x + dx, 4) * 4 + lax.rem(zh + dz, 4)

    other = dev(x, zh, 1 - c)
    z_up, z_down = dev(x, zh + 1, c), dev(x, zh - 1, c)
    x_up, x_down = dev(x + 1, zh, c), dev(x - 1, zh, c)
    barrier = pltpu.get_barrier_semaphore()
    for peer in (other, z_up, z_down, x_up, x_down):
        pl.semaphore_signal(barrier, inc=1, device_id=peer, device_id_type=MESH)
    pl.semaphore_wait(barrier, 5)

    sends = []

    def put(src, dst, sem, peer):
        copy = pltpu.make_async_remote_copy(
            src_ref=src, dst_ref=dst, send_sem=send.at[len(sends)], recv_sem=recv.at[sem],
            device_id=peer, device_id_type=MESH,
        )
        copy.start()
        sends.append(copy)

    def got(ref, sem):
        pltpu.make_async_remote_copy(
            src_ref=ref, dst_ref=ref, send_sem=send.at[0], recv_sem=recv.at[sem],
            device_id=other, device_id_type=MESH,
        ).wait_recv()

    home = slot(0, 0)
    put(own_slices, slices.at[home], 0, z_up)
    put(own_slices, slices.at[home], 1, z_down)
    put(own_slices, slices.at[home], 4, x_up)
    put(own_slices, slices.at[home], 5, x_down)
    img = pl.ds(pl.multiple_of(c * 16, 16), 16)
    put(own_images, images.at[:, img], 20, other)
    keep = pltpu.make_async_copy(own_slices, slices.at[home], local.at[0])
    keep.start()
    keep_images = pltpu.make_async_copy(own_images, images.at[:, img], local.at[1])
    keep_images.start()

    def along_x(dz):
        here = slices.at[slot(0, dz)]
        put(here, here, 4 + 4 * dz, x_up)
        put(here, here, 5 + 4 * dz, x_down)

    def pass_x(dz):
        below = slices.at[slot(3, dz)]
        got(below, 4 + 4 * dz)
        put(below.at[0], below.at[0], 6 + 4 * dz, x_up)
        above = slices.at[slot(1, dz)]
        got(above, 5 + 4 * dz)
        put(above.at[1], above.at[1], 7 + 4 * dz, x_down)

    below = slices.at[slot(0, 3)]
    got(below, 0)
    put(below.at[0], below.at[0], 2, z_up)
    along_x(3)
    above = slices.at[slot(0, 1)]
    got(above, 1)
    put(above.at[1], above.at[1], 3, z_down)
    along_x(1)
    pass_x(0)
    far = slices.at[slot(0, 2)]
    got(far.at[0], 2)
    got(far.at[1], 3)
    along_x(2)
    for dz in (3, 1, 2):
        pass_x(dz)
    for dz in range(4):
        far = slices.at[slot(2, dz)]
        got(far.at[0], 6 + 4 * dz)
        got(far.at[1], 7 + 4 * dz)
    got(images.at[:, pl.ds(pl.multiple_of((1 - c) * 16, 16), 16)], 20)
    keep.wait()
    keep_images.wait()
    for copy in sends:
        copy.wait_send()


def gather(images, slices):
    return pl.pallas_call(
        gather_kernel,
        out_shape=(
            jax.ShapeDtypeStruct((FREQ, IMGS, 256), BF16),
            jax.ShapeDtypeStruct((16, 2, FREQ, 256), BF16),
        ),
        in_specs=vmem(2),
        out_specs=vmem(2),
        scratch_shapes=[
            pltpu.SemaphoreType.DMA((21,)),
            pltpu.SemaphoreType.DMA((21,)),
            pltpu.SemaphoreType.DMA((2,)),
        ],
        compiler_params=params(collective_id=0, has_side_effects=True),
        name="gather_slices",
    )(images, slices)


def aligned_rows(pair, factors):
    real, imag = pair[:, :128], pair[:, 128:]
    rows = []
    for r in range(8):
        row = factors[r : r + 1]
        if r == 4:
            rows.append(jnp.zeros((IMGS, 256), F32))
        else:
            rows.append(jnp.concatenate([real * row, imag * row], axis=1))
    return rows


def scores_kernel(
    slices, images, weight, trig, sums, counts, expo_ref, stats_ref, real, imag, acc, energy
):
    sign = jnp.where(lax.broadcasted_iota(jnp.int32, (1, 128), 1) < 64, 1.0, -1.0).astype(F32)

    def widen(o, carry):
        block = slices[o].astype(F32)
        rows = pl.ds(pl.multiple_of(o * FREQ, FREQ), FREQ)
        real[rows, :] = block[:, :128]
        imag[rows, :] = block[:, 128:]
        return carry

    lax.fori_loop(0, ORI, widen, 0)
    acc[...] = jnp.zeros_like(acc)
    energy[...] = jnp.zeros_like(energy)

    def correlate(m, src):
        at = pl.ds(src, ORI, stride=FREQ)
        s_r, s_i = real[at, :], imag[at, :]
        w = weight[pl.ds(m, 1), :]
        energy[...] += w * (s_r * s_r + s_i * s_i)
        left = jnp.concatenate(
            [
                jnp.concatenate([s_r, s_i], axis=1),
                jnp.concatenate([-sign * s_i, sign * s_r], axis=1),
            ],
            axis=0,
        ).astype(BF16)
        rows = aligned_rows(images[src].astype(F32), trig[...] * w)
        high = [row.astype(BF16) for row in rows]
        low = [(row - top.astype(F32)).astype(BF16) for row, top in zip(rows, high)]
        dims = (((1,), (1,)), ((), ()))
        return lax.dot_general(
            left, jnp.concatenate(high, axis=0), dims, preferred_element_type=F32
        ) + lax.dot_general(left, jnp.concatenate(low, axis=0), dims, preferred_element_type=F32)

    def some(group, carry):
        parts = []
        for j in range(5):
            m = group * 5 + j
            parts.append((m, correlate(m, lax.rem(m, FREQ))))
        for b in range(4):
            for c in range(2):
                for half in range(2):
                    even = c == half
                    if b == 0 and not even:
                        continue
                    lanes = slice(half * 128, half * 128 + 128)
                    total = acc[b, c * ORI : (c + 1) * ORI, lanes]
                    for m, part in parts:
                        value = part[c * ORI : (c + 1) * ORI, lanes]
                        if b:
                            value = value * sums[m, pl.ds(b if even else 4 + b, 1), :]
                        total = total + value
                    acc[b, c * ORI : (c + 1) * ORI, lanes] = total
        return carry

    lax.fori_loop(0, STEPS // 5, some, 0)
    half_energy = 0.5 * jnp.sum(energy[...], axis=1, keepdims=True)
    peak = jnp.full((ORI, 128), -1e30, F32)
    for b in range(4):
        q1 = acc[b, :ORI, :128] - half_energy
        q2 = acc[b, :ORI, 128:]
        q4 = acc[b, ORI:, :128]
        q3 = acc[b, ORI:, 128:]
        for tau in (1, -1) if b else (1,):
            for sigma in (1, -1):
                entry = entry_of(sigma, tau * b)
                value = q1 - sigma * q3
                if b:
                    value = value - tau * (sigma * q2 + q4)
                expo_ref[entry] = value
                peak = jnp.maximum(peak, jnp.where(counts[pl.ds(entry, 1), :] > 0, value, -1e30))
    peak = jnp.max(peak, axis=0, keepdims=True)
    peak = jnp.maximum(peak, pltpu.roll(peak, 32, 1))
    peak = jnp.maximum(peak, pltpu.roll(peak, 64, 1))
    mass = jnp.zeros((ORI, 128), F32)
    for entry in range(14):
        count = counts[pl.ds(entry, 1), :]
        value = jnp.where(count > 0, expo_ref[entry] - peak, -1e30)
        value = jnp.exp(value) * count
        expo_ref[entry] = value
        mass = mass + value
    mass = jnp.sum(mass, axis=0, keepdims=True)
    mass = mass + pltpu.roll(mass, 32, 1)
    mass = mass + pltpu.roll(mass, 64, 1)
    stats_ref[...] = jnp.concatenate([peak, mass, jnp.zeros((6, 128), F32)], axis=0)


def entry_of(sigma, shift_y):
    return (0 if sigma > 0 else 7) + shift_y + 3


def scores(slices, images, weight, trig, sums, counts):
    return pl.pallas_call(
        scores_kernel,
        out_shape=(
            jax.ShapeDtypeStruct((14, ORI, 128), F32),
            jax.ShapeDtypeStruct((8, 128), F32),
        ),
        in_specs=vmem(6),
        out_specs=vmem(2),
        scratch_shapes=[
            pltpu.VMEM((ORI * FREQ, 128), F32),
            pltpu.VMEM((ORI * FREQ, 128), F32),
            pltpu.VMEM((4, 2 * ORI, 256), F32),
            pltpu.VMEM((ORI, 128), F32),
        ],
        compiler_params=params(),
        name="score_images",
    )(slices, images, weight, trig, sums, counts)


def stats_kernel(own, every, send, recv, local):
    x, zh, c, ori = place()
    me = ori * 2 + c

    def dev(index):
        return (x * 8 + zh * 2 + index % 2, index // 2)

    barrier = pltpu.get_barrier_semaphore()
    for step in range(1, 32):
        peer = dev(lax.rem(me + step, 32))
        pl.semaphore_signal(barrier, inc=1, device_id=peer, device_id_type=MESH)
    keep = pltpu.make_async_copy(own, every.at[0], local)
    keep.start()
    pl.semaphore_wait(barrier, 31)
    copies = []
    for step in range(1, 32):
        copies.append(
            pltpu.make_async_remote_copy(
                src_ref=own, dst_ref=every.at[step], send_sem=send.at[step],
                recv_sem=recv.at[step], device_id=dev(lax.rem(me + step, 32)), device_id_type=MESH,
            )
        )
        copies[-1].start()
    keep.wait()
    for copy in copies:
        copy.wait()


def exchange(stats):
    return pl.pallas_call(
        stats_kernel,
        out_shape=jax.ShapeDtypeStruct((32, 8, 128), F32),
        in_specs=vmem(1),
        out_specs=pl.BlockSpec(memory_space=pltpu.VMEM),
        scratch_shapes=[
            pltpu.SemaphoreType.DMA((32,)),
            pltpu.SemaphoreType.DMA((32,)),
            pltpu.SemaphoreType.DMA,
        ],
        compiler_params=params(collective_id=1, has_side_effects=True),
        name="exchange_stats",
    )(stats)


def insert_kernel(
    every, expo, images, weight, trig, sums, kernels, codes,
    volume_ref, loglik_ref, post, folded, inserted, chosen,
):
    sign = jnp.where(lax.broadcasted_iota(jnp.int32, (1, 128), 1) < 64, 1.0, -1.0).astype(F32)
    low = lax.broadcasted_iota(jnp.int32, (2 * ORI, 128), 1) < 64

    place_row = lax.broadcasted_iota(jnp.int32, (512, 128), 0)

    def choose(k, carry):
        for j in range(16):
            hit = place_row == codes[pl.ds(j, 1), :] - k * 512
            rows = pl.ds(pl.multiple_of(k * 512, 512), 512)
            chosen[rows, j * 128 : j * 128 + 128] = jnp.where(hit, 1.0, 0.0).astype(BF16)
        return carry

    lax.fori_loop(0, 3, choose, 0)

    peaks, masses = every[:, 0, :], every[:, 1, :]
    peak = jnp.max(peaks, axis=0, keepdims=True)
    mass = jnp.sum(masses * jnp.exp(peaks - peak), axis=0, keepdims=True)
    loglik_ref[...] = jnp.broadcast_to(peak + jnp.log(mass), (8, 128))
    scale = jnp.exp(peaks[0:1] - peak) / mass
    for b in range(4):
        q1 = jnp.zeros((ORI, 128), F32)
        q2, q3, q4 = q1, q1, q1
        for tau in (1, -1) if b else (1,):
            for sigma in (1, -1):
                value = expo[entry_of(sigma, tau * b)] * scale
                q1 = q1 + value
                q2 = q2 - (sigma * tau) * value
                q3 = q3 - sigma * value
                q4 = q4 - tau * value
        post[b, :ORI, :128] = q1
        post[b, :ORI, 128:] = q2
        post[b, ORI:, :128] = q4
        post[b, ORI:, 128:] = q3

    def back(m, src):
        w = weight[pl.ds(m, 1), :]
        rows = aligned_rows(images[src].astype(F32), trig[...] * w)
        right = jnp.concatenate([row.astype(BF16) for row in rows], axis=0)
        parts = []
        for c in range(2):
            halves = []
            for half in range(2):
                even = c == half
                lanes = slice(half * 128, half * 128 + 128)
                total = None
                for b in range(4):
                    if b == 0 and not even:
                        continue
                    value = post[b, c * ORI : (c + 1) * ORI, lanes]
                    if b:
                        value = value * sums[m, pl.ds(b if even else 4 + b, 1), :]
                    total = value if total is None else total + value
                halves.append(total)
            parts.append(jnp.concatenate(halves, axis=1))
        left = jnp.concatenate(parts, axis=0).astype(BF16)
        grad = jnp.dot(left, right, preferred_element_type=F32)
        real = grad[:ORI, :128] + sign * grad[ORI:, 128:]
        imag = grad[:ORI, 128:] - sign * grad[ORI:, :128]
        return jnp.concatenate([real, imag], axis=0)

    def some_back(group, carry):
        for j in range(4):
            m = group * 4 + j
            folded[m] = back(m, m)
        return carry

    lax.fori_loop(0, FREQ // 4, some_back, 0)
    folded[0] = folded[0] + back(FREQ, 0)

    def insert(block, first, second):
        value = jnp.where(low, first, second)
        high = value.astype(BF16)
        rest = (value - high.astype(F32)).astype(BF16)
        out = jnp.dot(
            jnp.concatenate([high, rest], axis=0), kernels[block], preferred_element_type=F32
        )
        out = out[: 2 * ORI] + out[2 * ORI :]
        rows = pl.ds(pl.multiple_of(block * ORI, ORI), ORI)
        inserted[rows, :] = jnp.concatenate([out[:ORI], out[ORI:]], axis=1).astype(BF16)

    def some_insert(group, carry):
        for j in range(2):
            b = group * 2 + j
            insert(32 + b, folded[2 * b], pltpu.roll(folded[2 * b + 1], 64, 1))
            m = FREQ - 2 * b
            insert(b, pltpu.roll(folded[lax.rem(m, FREQ)], 64, 1), folded[m - 1])
        return carry

    lax.fori_loop(0, 16, some_insert, 0)

    def total(t, carry):
        k, part = t // 2, t % 2
        rows = pl.ds(pl.multiple_of(t * 256, 256), 256)
        sums_here = jnp.dot(chosen[rows, :], inserted[...], preferred_element_type=F32)
        volume_ref[k, pl.ds(pl.multiple_of(part * 256, 256), 256), :] = sums_here
        return carry

    lax.fori_loop(0, 6, total, 0)


def insert(every, expo, images, weight, trig, sums, kernels, codes):
    return pl.pallas_call(
        insert_kernel,
        out_shape=(
            jax.ShapeDtypeStruct((3, 512, 256), F32),
            jax.ShapeDtypeStruct((8, 128), F32),
        ),
        in_specs=vmem(8),
        out_specs=vmem(2),
        scratch_shapes=[
            pltpu.VMEM((4, 2 * ORI, 256), F32),
            pltpu.VMEM((FREQ, 2 * ORI, 128), F32),
            pltpu.VMEM((FREQ * ORI, 256), BF16),
            pltpu.VMEM((1536, 2048), BF16),
        ],
        compiler_params=params(),
        name="insert_slices",
    )(every, expo, images, weight, trig, sums, kernels, codes)


def reduce_kernel(
    part, out_ref, cores, x_out, x_in, x_own, z_out, z_in, z_own, y_out, y_in, send, recv
):
    x, zh, c, ori = place()
    y, zl = ori // 2, ori % 2
    z = zh * 2 + zl

    def dev(xx, zz, cc, yy):
        return (xx * 8 + (zz // 2) * 2 + cc, yy * 2 + zz % 2)

    core_peer = dev(x, z, 1 - c, y)
    x_peers = [dev(lax.rem(x + s, 4), z, c, y) for s in range(1, 4)]
    z_peers = [dev(x, lax.rem(z + s, 8), c, y) for s in range(1, 8)]
    y_peers = [dev(x, z, c, lax.rem(y + s, 8)) for s in range(1, 8)]
    barrier = pltpu.get_barrier_semaphore()
    for peer in [core_peer] + x_peers + z_peers + y_peers:
        pl.semaphore_signal(barrier, inc=1, device_id=peer, device_id_type=MESH)
    pl.semaphore_wait(barrier, 18)

    def put(src, dst, sem, peer):
        copy = pltpu.make_async_remote_copy(
            src_ref=src, dst_ref=dst, send_sem=send.at[sem], recv_sem=recv.at[sem],
            device_id=peer, device_id_type=MESH,
        )
        copy.start()
        return copy

    def half(cc):
        return pl.ds(pl.multiple_of(cc * 256, 256), 256)

    sent = [put(part.at[:, half(1 - c)], cores, 0, core_peer)]
    sent[0].wait_recv()
    for k in range(3):
        total = part[k, half(c), :] + cores[k]
        x_out[:, k * 256 : k * 256 + 256] = total.astype(BF16)
        cores[k] = total

    def chunk(xx):
        return pl.ds(pl.multiple_of(xx * 64, 64), 64)

    steps = [
        put(x_out.at[chunk(lax.rem(x + s, 4))], x_in.at[s - 1], s, x_peers[s - 1])
        for s in range(1, 4)
    ]
    for copy in steps:
        copy.wait_recv()
    sent += steps
    for k in range(3):
        lanes = slice(k * 256, k * 256 + 256)
        total = cores[k, chunk(x), :]
        for s in range(3):
            total = total + x_in[s, :, lanes].astype(F32)
        x_own[:, lanes] = total
    for zz in range(8):
        rows = x_own[zz * 8 : zz * 8 + 8, :]
        rows = jnp.concatenate([rows[:, :384], rows[:, 384:]], axis=0)
        z_own[zz] = rows
        z_out[zz] = rows.astype(BF16)
    steps = [
        put(z_out.at[lax.rem(z + s, 8)], z_in.at[s - 1], 3 + s, z_peers[s - 1])
        for s in range(1, 8)
    ]
    for copy in steps:
        copy.wait_recv()
    sent += steps
    total = z_own[z]
    for s in range(7):
        total = total + z_in[s].astype(F32)
    for yy in range(8):
        for j in range(6):
            row = (j // 3) * 8 + yy
            y_out[yy, j : j + 1, :] = total[row : row + 1, (j % 3) * 128 : (j % 3) * 128 + 128]
        y_out[yy, 6:8, :] = jnp.zeros((2, 128), F32)
    steps = [
        put(y_out.at[lax.rem(y + s, 8)], y_in.at[s - 1], 10 + s, y_peers[s - 1])
        for s in range(1, 8)
    ]
    for copy in steps:
        copy.wait_recv()
    sent += steps
    total = y_out[y]
    for s in range(7):
        total = total + y_in[s]
    out_ref[...] = total
    for copy in sent:
        copy.wait_send()


def reduce(part):
    return pl.pallas_call(
        reduce_kernel,
        out_shape=jax.ShapeDtypeStruct((8, 128), F32),
        in_specs=vmem(1),
        out_specs=pl.BlockSpec(memory_space=pltpu.VMEM),
        scratch_shapes=[
            pltpu.VMEM((3, 256, 256), F32),
            pltpu.VMEM((256, 768), BF16),
            pltpu.VMEM((3, 64, 768), BF16),
            pltpu.VMEM((64, 768), F32),
            pltpu.VMEM((8, 16, 384), BF16),
            pltpu.VMEM((7, 16, 384), BF16),
            pltpu.VMEM((8, 16, 384), F32),
            pltpu.VMEM((8, 8, 128), F32),
            pltpu.VMEM((7, 8, 128), F32),
            pltpu.SemaphoreType.DMA((18,)),
            pltpu.SemaphoreType.DMA((18,)),
        ],
        compiler_params=params(collective_id=2, has_side_effects=True),
        name="reduce_volume",
    )(part)


def fold(raw):
    return pl.pallas_call(
        fold_kernel,
        out_shape=(
            jax.ShapeDtypeStruct((FREQ, 16, 256), BF16),
            jax.ShapeDtypeStruct((2, FREQ, 256), BF16),
        ),
        in_specs=vmem(1),
        out_specs=vmem(2),
        scratch_shapes=[pltpu.VMEM((2, FREQ, 256), F32)],
        compiler_params=params(),
        name="fold_rows",
    )(raw)


def weight_rows(noise_weight):
    grid = noise_weight.reshape(128, 64)
    up = grid[64:]
    down = jnp.concatenate([jnp.zeros((1, 64), F32), grid[63:0:-1]], axis=0)
    body = jnp.concatenate([up, down], axis=1)
    last = jnp.concatenate([jnp.zeros((64,), F32), grid[0]])[None]
    return jnp.concatenate([body, last, jnp.zeros((7, 128), F32)], axis=0)


def cell_counts(shifts):
    size = jnp.arange(4)
    side = jnp.array([1, -1])
    shift_y = jnp.arange(-3, 4)
    col = side[:, None] * size[None, :]
    live = (side[:, None] > 0) | (size[None, :] > 0)
    hit = (
        (shifts[:, 0][:, None, None, None] == col[None, :, None, :])
        & (shifts[:, 1][:, None, None, None] == shift_y[None, None, :, None])
        & live[None, :, None, :]
    )
    count = jnp.sum(hit.astype(F32), axis=0).reshape(14, 4)
    count = jnp.broadcast_to(count[:, :, None], (14, 4, IMGS)).reshape(14, 128)
    return jnp.concatenate([count, jnp.zeros((2, 128), F32)], axis=0)


def target_codes(targets, core):
    own = lax.dynamic_index_in_dim(targets.reshape(16, 2, 2, 64), core, 1, keepdims=False)
    own = own.reshape(ORI, 64).T
    owner, k = own // 3, own % 3
    core_at = (owner // 16) % 2
    z_hi = (owner // 32) % 4
    x = owner // 128
    y = (owner // 2) % 8
    z = z_hi * 2 + owner % 2
    row = ((core_at * 4 + x) * 8 + z) * 8 + y
    return (k * 512 + row).reshape(16, 128)


def shards(images, slices, noise_weight, shifts, kernels, targets):
    core = lax.axis_index("dom") % 2
    trig, sums = (jnp.asarray(t) for t in tables())
    raw = jnp.concatenate([images.reshape(16, 2 * PIX), slices.reshape(2, 2 * PIX)], axis=0)
    weight = weight_rows(noise_weight)
    counts = cell_counts(shifts)
    codes = target_codes(targets, core)
    own_images, own_slices = fold(raw)
    all_images, all_slices = gather(own_images, own_slices)
    all_slices = all_slices.reshape(ORI, FREQ, 256)
    expo, stats = scores(all_slices, all_images, weight, trig, sums, counts)
    every = exchange(stats)
    part, loglik = insert(every, expo, all_images, weight, trig, sums, kernels, codes)
    volume = reduce(part)
    loglik = lax.dynamic_slice_in_dim(loglik[0], core * 16, 16)
    return volume[:6].reshape(3, 2, 128), loglik


def solution(mesh):
    placed = (
        P("dom", None, None),
        P(("orient", "dom"), None, None),
        P(),
        P(),
        P(),
        P("orient", None),
    )
    return jax.shard_map(
        shards,
        mesh=mesh,
        in_specs=placed,
        out_specs=(P(("dom", "orient"), None, None), P("dom")),
        check_vma=False,
    )
```

time: 635 us -> 115 us (0.18)
  waiting for transfers between devices: 356 us -> 0 us
  Pallas kernels: 0 us -> 98.9 us
  local copies, waits for them, and re-layouts: 89.1 us -> 9.6 us
  other arithmetic: 67.1 us -> 5 us
  matrix products: 53.3 us -> 0 us
  blocking collectives: 49.4 us -> 0 us
  between operations: 14.1 us -> 0.72 us
    unnamed x3 -> x0, waiting for transfers between devices: 288 us -> none
    pallas_call x0 -> x6, Pallas kernels: none -> 98.9 us  [the longest x1 26.9 us: reduce(): pl.pallas_call(reduce_kernel, out_shape=jax.ShapeDtypeStruct((8, 128), F3...]
    all_gather x1 -> x0, waiting for transfers between devices: 67.2 us -> none  [shards(): piece = lax.all_gather(slices, 'dom', axis=0, tiled=True)]
    dot_general x15 -> x0, matrix products: 53.3 us -> none  [the longest x7 41.1 us: back_group(): lax.dot_general(weights, aligned, (((0,), (0,)), ((), ())), preferred_ele...]
    while x22 -> x0, local copies, waits for them, and re-layouts: 38 us -> none
    another operation x8 -> x0, local copies, waits for them, and re-layouts: 27.5 us -> none  [the longest x7 26.7 us: align_images(): return jnp.stack([out_real, out_imag], axis=2).astype(jnp.bfloat16)]
    pmax x1 -> x0, blocking collectives: 25.6 us -> none  [shards(): peak = lax.pmax(local_peak, 'orient')]
    scatter-add x1 -> x0, other arithmetic: 25.2 us -> none  [shards(): jax.ops.segment_sum(inserted, targets.reshape(-1), num_segments=total_blo...]
  transfers between devices with their start and end apart: 2 -> 0, of which waited for: 2 -> 0; matrix products, arithmetic and copies ran while one was open for 0% -> 0% of each run, Pallas kernels for 0% -> 0%
where the time goes in v1:
time: 115 us; the launch traced here: 114 us
  Pallas kernels  98.9 us (86%)
  local copies, waits for them, and re-layouts  9.6 us (8%)
  other arithmetic  5 us (4%)
    pallas_call x1, Pallas kernels, reduce(): pl.pallas_call(reduce_kernel, out_shape=jax.ShapeDtypeStruct((8, 128), F3...  26.9 us
    pallas_call x1, Pallas kernels, gather(): pl.pallas_call(gather_kernel, out_shape=(jax.ShapeDtypeStruct((FREQ, IMGS...  25.8 us
    pallas_call x1, Pallas kernels, exchange(): pl.pallas_call(stats_kernel, out_shape=jax.ShapeDtypeStruct((32, 8, 128),...  17.6 us
    pallas_call x1, Pallas kernels, insert(): pl.pallas_call(insert_kernel, out_shape=(jax.ShapeDtypeStruct((3, 512, 25...  15.7 us
    pallas_call x1, Pallas kernels, scores(): pl.pallas_call(scores_kernel, out_shape=(jax.ShapeDtypeStruct((14, ORI, 1...  10.7 us

profile of v1, /device:TPU:1, one launch (start us, length us, event | category | flops | bytes accessed | tf_op | source)
XLA Modules:
  0.0 114.2 jit_solution(10458196183969498067)
XLA Ops:
  0.6 0.7 slice.48
  1.3 0.1 pad_bitcast_fusion
  1.4 0.1 pad.6.clone
  1.5 0.7 broadcast_or_fusion
  2.2 0.7 iota_multiply_fusion
  3.0 0.8 slice_bitcast_fusion.1
  3.7 0.1 broadcast_compare_fusion.1
  3.8 0.1 broadcast_compare_fusion
  3.9 0.2 convert_reduce_fusion
  4.0 0.7 fusion.19
  4.8 0.7 slice.44
  5.5 0.1 slice.45
  5.6 0.8 slice.46
  6.4 0.1 slice.47
  6.5 0.7 fusion.1.weight
  7.2 0.1 broadcast_in_dim.11
  7.3 0.1 reshape.155
  7.4 0.6 concatenate.23.counts
  8.0 0.7 bitcast_divide_fusion
  8.7 0.1 fusion.4
  8.8 0.1 copy.21
  8.9 0.7 reshape.157.codes
  9.6 0.9 copy.24
  10.5 1.3 %copy.23 = bf16[2,8,2,8192]{3,1,2,0:T(8,128)(2,1)S(1)} copy(bf16[2,8,2,8192]{3,2,1,0:T(2,128)(2,1)} %bitcast.37) | data formatting | bytes 1048576
  11.8 1.0 pad_maximum_fusion.raw_ref
  12.8 2.3 %fold_rows.1 = (bf16[64,16,256]{2,1,0:T(8,128)(2,1)}, bf16[2,64,256]{2,1,0:T(8,128)(2,1)}) custom-call(bf16[18,16384]{1,0:T(8,128)(2,1)} %pad_maximum_fusion.raw_ref), custom_call_target="tpu_custom_call" | custom-call | tf_op jit(solution)/shard_map/fold_rows/pallas_call | solution.py:587
  15.1 25.8 %gather_slices.1 = (bf16[64,32,256]{2,1,0:T(8,128)(2,1)}, bf16[16,2,64,256]{3,2,1,0:T(8,128)(2,1)}) custom-call(bf16[64,16,256]{2,1,0:T(8,128)(2,1)} %get-tuple-element.10.own_images, bf16[2,64,256]{2,1,0:T(8,128)(2,1)} %get-tuple-element.11.own_slices), custom_call_target="tpu_custom_call" | custom-call | tf_op jit(solution)/shard_map/gather_slices/pallas_call | solution.py:163
  40.9 10.7 %score_images.1 = (f32[14,32,128]{2,1,0:T(8,128)}, f32[8,128]{1,0:T(8,128)}) custom-call(bf16[32,64,256]{2,1,0:T(8,128)(2,1)} %bitcast.36, bf16[64,32,256]{2,1,0:T(8,128)(2,1)} %get-tuple-element.13.images, f32[72,128]{1,0:T(8,128)} %fusion.1.weight, f32[8,128]{1,0:T(8,128)} %constant.136.clone.trig, f32[65,8,128]{2,1,0:T(8,128)} %constant.137.clone.sums, ...), custom_call_target="tpu_custom_call" | custom-call | tf_op jit(solution)/shard_map/score_images/pallas_call | solution.py:287
  51.5 17.6 %exchange_stats.1.every = f32[32,8,128]{2,1,0:T(8,128)} custom-call(f32[8,128]{1,0:T(8,128)} %get-tuple-element.14.own), custom_call_target="tpu_custom_call" | custom-call | tf_op jit(solution)/shard_map/exchange_stats/pallas_call | solution.py:335
  69.2 15.7 %insert_slices.1 = (f32[3,512,256]{2,1,0:T(8,128)}, f32[8,128]{1,0:T(8,128)}) custom-call(f32[32,8,128]{2,1,0:T(8,128)} %exchange_stats.1.every, f32[14,32,128]{2,1,0:T(8,128)} %get-tuple-element.15.expo, bf16[64,32,256]{2,1,0:T(8,128)(2,1)} %get-tuple-element.13.images, f32[72,128]{1,0:T(8,128)} %fusion.1.weight, f32[8,128]{1,0:T(8,128)} %constant.136.clone.trig, ...), custom_call_target="tpu_custom_call" | custom-call | tf_op jit(solution)/shard_map/insert_slices/pallas_call | solution.py:455
  84.8 26.9 %reduce_volume.1 = f32[8,128]{1,0:T(8,128)} custom-call(f32[3,512,256]{2,1,0:T(8,128)} %get-tuple-element.16.part), custom_call_target="tpu_custom_call" | custom-call | tf_op jit(solution)/shard_map/reduce_volume/pallas_call | solution.py:563
  111.7 1.3 %reshape.158 = f32[3,2,128]{2,1,0:T(2,128)} reshape(f32[6,128]{1,0:T(8,128)} %bitcast.44) | data formatting | bytes 6144 | tf_op jit(solution)/shard_map/reshape | solution.py:654
  113.0 0.7 slice.52
  113.6 0.6 dynamic-slice_bitcast_fusion
  (6 shorter events, 0.1 us)

commit v2 on v0

v2 whole, which is shorter than its diff:
```python
import jax
import jax.numpy as jnp
import numpy as np
from jax import lax
from jax.experimental import pallas as pl
from jax.experimental.pallas import tpu as pltpu
from jax.sharding import PartitionSpec as P

F32 = jnp.float32
BF16 = jnp.bfloat16
MESH = pl.DeviceIdType.MESH
PIX = 8192
TRANS = 49
FREQ = 64
IMGS = 32
ORI = 32
STEPS = FREQ + 1
VMEM_LIMIT = 56 * 1024 * 1024


def tables():
    kx = np.arange(64)
    unit = 2.0 * np.pi / 128.0
    rows = np.zeros((8, 128), np.float32)
    for a in range(4):
        rows[a, :64] = rows[a, 64:] = np.cos(unit * a * kx)
    for a in range(1, 4):
        rows[4 + a, :64] = np.sin(unit * a * kx)
        rows[4 + a, 64:] = -np.sin(unit * a * kx)
    m = np.arange(STEPS)
    sums = np.zeros((STEPS, 8, 128), np.float32)
    for b in range(4):
        sums[:, b, :] = np.cos(unit * b * m)[:, None]
        sums[:, 4 + b, :] = np.where(m == 64, 0.0, np.sin(unit * b * m))[:, None]
    return rows, sums


def entry_of(sigma, shift_y):
    return (0 if sigma > 0 else 7) + shift_y + 3


def fold_pair(m, block, low):
    if m % 2 == 0:
        first = block(32 + m // 2)
        second = pltpu.roll(block(32 - m // 2 if m else 0), 64, 1)
    else:
        first = pltpu.roll(block(32 + (m - 1) // 2), 64, 1)
        second = block(32 - (m + 1) // 2)
    return jnp.where(low, first, second)


def aligned_rows(pair, factors):
    real, imag = pair[:, :128], pair[:, 128:]
    rows = []
    for r in range(8):
        row = factors[r : r + 1]
        if r == 4:
            rows.append(jnp.zeros((IMGS, 256), F32))
        else:
            rows.append(jnp.concatenate([real * row, imag * row], axis=1))
    return rows


def merge_stats(stats):
    peak = stats[0][0:1]
    for part in stats[1:]:
        peak = jnp.maximum(peak, part[0:1])
    mass = jnp.zeros_like(peak)
    for part in stats:
        mass = mass + part[1:2] * jnp.exp(part[0:1] - peak)
    return peak, mass


def step_kernel(
    images_hbm, slices_hbm, noise_weight, shifts, kernels_hbm, targets, trig, sums,
    volume_ref, loglik_ref,
    images_raw, slices_raw, kernels,
    fold_rows, image_real, image_imag, images, slices, weight, high, low_part, real, imag, energy, acc, expo,
    counts, codes, chosen, post, back, folded, inserted, part, cores,
    stats_own, stats_near, stats_mid, stats_far,
    x_out, x_in, x_own, z_out, z_in, z_own, y_out, y_in,
    send, recv, local,
):
    dom, ori = lax.axis_index("dom"), lax.axis_index("orient")
    c, zh, x = dom % 2, (dom // 2) % 4, dom // 8
    y, zl = ori // 2, ori % 2
    z = zh * 2 + zl

    def dev(dx, dz, dc, dy):
        xx, zz, yy = lax.rem(x + dx, 4), lax.rem(z + dz, 8), lax.rem(y + dy, 8)
        cc = 1 - c if dc else c
        return (xx * 8 + (zz // 2) * 2 + cc, yy * 2 + zz % 2)

    def dev_zl(dl, dc):
        cc = 1 - c if dc else c
        ll = 1 - zl if dl else zl
        return (x * 8 + zh * 2 + cc, y * 2 + ll)

    core_peer = dev(0, 0, 1, 0)
    x_peers = [dev(s, 0, 0, 0) for s in range(1, 4)]
    z_peers = [dev(0, s, 0, 0) for s in range(1, 8)]
    y_peers = [dev(0, 0, 0, s) for s in range(1, 8)]
    near_peers = [core_peer, dev_zl(1, 0), dev_zl(1, 1)]
    barrier = pltpu.get_barrier_semaphore()
    everyone = [core_peer, near_peers[2]] + x_peers + z_peers + y_peers
    for peer in everyone:
        pl.semaphore_signal(barrier, inc=1, device_id=peer, device_id_type=MESH)

    get_slices = pltpu.make_async_copy(slices_hbm, slices_raw, local.at[0])
    get_slices.start()
    get_images = pltpu.make_async_copy(images_hbm, images_raw, local.at[1])
    get_images.start()
    get_kernels = pltpu.make_async_copy(kernels_hbm, kernels, local.at[2])
    get_kernels.start()

    sends = []

    def put(src, dst, sem, peer):
        copy = pltpu.make_async_remote_copy(
            src_ref=src, dst_ref=dst, send_sem=send.at[sem], recv_sem=recv.at[sem],
            device_id=peer, device_id_type=MESH,
        )
        copy.start()
        sends.append(copy)
        return copy

    def got(ref, sem):
        pltpu.make_async_remote_copy(
            src_ref=ref, dst_ref=ref, send_sem=send.at[sem], recv_sem=recv.at[sem],
            device_id=core_peer, device_id_type=MESH,
        ).wait_recv()

    low = lax.broadcasted_iota(jnp.int32, (1, 128), 1) < 64
    sign = jnp.where(low, 1.0, -1.0).astype(F32)

    home = x * 4 + zh
    get_slices.wait()
    for j in range(2):
        for m in range(FREQ):
            both = fold_pair(
                m, lambda b: slices_raw[j, :, b * 128 : b * 128 + 128].astype(F32), low
            )
            fold_rows[m : m + 1, :128] = both[0:1]
            fold_rows[m : m + 1, 128:] = both[1:2]
        slices[home, j] = fold_rows[...].astype(BF16)

    def fold_images(first, count):
        def one(i, carry):
            for m in range(FREQ):
                both = fold_pair(
                    m, lambda b: images_raw[i, :, b * 128 : b * 128 + 128].astype(F32), low
                )
                row = pl.ds(m * 16 + i, 1)
                image_real[row, :] = both[0:1]
                image_imag[row, :] = both[1:2]
            return carry

        lax.fori_loop(first, first + count, one, 0)

    def image_half(cc):
        return pl.ds(pl.multiple_of(cc * 16, 16), 16)

    def send_images():
        def one(m, carry):
            at = pl.ds(pl.multiple_of(m * 16, 16), 16)
            rows = jnp.concatenate([image_real[at, :], image_imag[at, :]], axis=1)
            images[m, image_half(c), :] = rows.astype(BF16)
            return carry

        lax.fori_loop(0, FREQ, one, 0)
        here = images.at[:, image_half(c)]
        put(here, here, 0, core_peer)

    def fold_weight():
        for m in range(FREQ):
            row = fold_pair(m, lambda b: noise_weight[b : b + 1, :], low)
            if m == 0:
                weight[FREQ : FREQ + 1, :] = jnp.where(low, 0.0, row)
                row = jnp.where(low, row, 0.0)
            weight[m : m + 1, :] = row

    def count_cells():
        row = lax.broadcasted_iota(jnp.int32, (16, 128), 0)
        size = lax.broadcasted_iota(jnp.int32, (16, 128), 1) // IMGS
        total = jnp.zeros((16, 128), F32)
        for t in range(TRANS):
            shift_x, shift_y = shifts[t, 0], shifts[t, 1]
            at = jnp.where(shift_x >= 0, 3, 10) + shift_y
            hit = (row == at) & (size == jnp.abs(shift_x))
            total = total + jnp.where(hit, 1.0, 0.0)
        counts[...] = total

    def find_codes():
        block = targets[...]
        owner = (block * 43691) >> 17
        k = block - 3 * owner
        core_at, z_hi_at, x_at = (owner >> 4) & 1, (owner >> 5) & 3, owner >> 7
        y_at, z_lo_at = (owner >> 1) & 7, owner & 1
        code = (core_at * 4 + x_at) * 192 + k * 64 + (z_hi_at * 2 + z_lo_at) * 8 + y_at
        orient = lax.broadcasted_iota(jnp.int32, (64, ORI), 0)
        mine = lax.broadcasted_iota(jnp.int32, (64, ORI), 1)
        pick = orient == (mine // 2) * 4 + c * 2 + mine % 2
        pick = jnp.where(pick, 1.0, 0.0).astype(BF16)
        dims = (((0,), (0,)), ((), ()))
        upper, lower = (code >> 5).astype(F32), (code & 31).astype(F32)
        upper = lax.dot_general(upper.astype(BF16), pick, dims, preferred_element_type=F32)
        lower = lax.dot_general(lower.astype(BF16), pick, dims, preferred_element_type=F32)
        code = upper * 32.0 + lower
        codes[...] = jnp.concatenate([code[16 * q : 16 * q + 16] for q in range(4)], axis=1)

    def choose(first, count):
        def one(t, carry):
            rows = lax.broadcasted_iota(jnp.int32, (128, 128), 0).astype(F32)
            rows = rows + (t * 128).astype(F32)
            at = pl.ds(pl.multiple_of(t * 128, 128), 128)
            for j in range(16):
                hit = rows == codes[j : j + 1, :]
                chosen[at, j * 128 : j * 128 + 128] = jnp.where(hit, 1.0, 0.0).astype(BF16)
            return carry

        lax.fori_loop(first, first + count, one, 0)

    def wait_images():
        got(images.at[:, image_half(1 - c)], 0)

    def align(first, count):
        def one(m, carry):
            factors = trig[...] * weight[pl.ds(m, 1), :]
            rows = aligned_rows(images[lax.rem(m, FREQ)].astype(F32), factors)
            for r, row in enumerate(rows):
                top = row.astype(BF16)
                high[m, r * IMGS : (r + 1) * IMGS, :] = top
                low_part[m, r * IMGS : (r + 1) * IMGS, :] = (row - top.astype(F32)).astype(BF16)
            return carry

        lax.fori_loop(first, first + count, one, 0)

    def slot(dx, dz):
        return lax.rem(x + dx, 4) * 4 + lax.rem(zh + dz, 4)

    def piece(dx, dz, h):
        return slices.at[slot(dx, dz), :, pl.ds(h * 32, 32)]

    def single(dx, dz, h, j):
        return slices.at[slot(dx, dz), j, pl.ds(h * 32, 32)]

    def gsem(kind, h):
        return 1 + kind * 2 + h

    z_up, z_down, x_up, x_down = z_peers[1], z_peers[5], x_peers[0], x_peers[2]

    def along_z(h):
        here = piece(0, 0, h)
        put(here, here, gsem(0, h), z_up)
        put(here, here, gsem(1, h), z_down)

    def along_x(dz, h):
        here = piece(0, dz, h)
        put(here, here, gsem(4 + 4 * dz, h), x_up)
        put(here, here, gsem(5 + 4 * dz, h), x_down)

    def pass_z(h):
        got(piece(0, 3, h), gsem(0, h))
        half = single(0, 3, h, 0)
        put(half, half, gsem(2, h), z_up)
        along_x(3, h)
        got(piece(0, 1, h), gsem(1, h))
        half = single(0, 1, h, 1)
        put(half, half, gsem(3, h), z_down)
        along_x(1, h)

    def far_z(h):
        got(single(0, 2, h, 0), gsem(2, h))
        got(single(0, 2, h, 1), gsem(3, h))
        along_x(2, h)

    def pass_x(dz, h):
        got(piece(3, dz, h), gsem(4 + 4 * dz, h))
        half = single(3, dz, h, 0)
        put(half, half, gsem(6 + 4 * dz, h), x_up)
        got(piece(1, dz, h), gsem(5 + 4 * dz, h))
        half = single(1, dz, h, 1)
        put(half, half, gsem(7 + 4 * dz, h), x_down)

    def far_x(dz, h):
        got(single(2, dz, h, 0), gsem(6 + 4 * dz, h))
        got(single(2, dz, h, 1), gsem(7 + 4 * dz, h))

    get_images.wait()
    fold_images(0, 4)
    pl.semaphore_wait(barrier, len(everyone))
    for h in range(2):
        along_z(h)
        along_x(0, h)
    fold_images(4, 6)
    pass_x(0, 0)
    pass_x(0, 1)
    pass_z(0)
    pass_z(1)
    fold_images(10, 6)
    send_images()
    pass_x(3, 0)
    pass_x(1, 0)
    far_z(0)
    fold_weight()
    pass_x(3, 1)
    pass_x(1, 1)
    far_z(1)
    wait_images()
    align(0, 20)
    pass_x(2, 0)
    pass_x(2, 1)
    align(20, 45)
    count_cells()
    find_codes()
    choose(0, 12)

    acc[...] = jnp.zeros_like(acc)
    energy[...] = jnp.zeros_like(energy)

    def widen(h):
        def one(o, carry):
            block = slices[o // 2, lax.rem(o, 2), pl.ds(h * 32, 32), :].astype(F32)
            rows = pl.ds(pl.multiple_of(o * FREQ + h * 32, 32), 32)
            real[rows, :] = block[:, :128]
            imag[rows, :] = block[:, 128:]
            return carry

        lax.fori_loop(0, ORI, one, 0)

    def correlate(m, src):
        at = pl.ds(src, ORI, stride=FREQ)
        s_r, s_i = real[at, :], imag[at, :]
        energy[...] += weight[pl.ds(m, 1), :] * (s_r * s_r + s_i * s_i)
        left = jnp.concatenate(
            [
                jnp.concatenate([s_r, s_i], axis=1),
                jnp.concatenate([-sign * s_i, sign * s_r], axis=1),
            ],
            axis=0,
        ).astype(BF16)
        dims = (((1,), (1,)), ((), ()))
        return lax.dot_general(
            left, high[m], dims, preferred_element_type=F32
        ) + lax.dot_general(left, low_part[m], dims, preferred_element_type=F32)

    def add_scores(parts):
        for b in range(4):
            for k in range(2):
                for half in range(2):
                    even = k == half
                    if b == 0 and not even:
                        continue
                    lanes = slice(half * 128, half * 128 + 128)
                    total = acc[b, k * ORI : (k + 1) * ORI, lanes]
                    for m, value in parts:
                        value = value[k * ORI : (k + 1) * ORI, lanes]
                        if b:
                            value = value * sums[m, pl.ds(b if even else 4 + b, 1), :]
                        total = total + value
                    acc[b, k * ORI : (k + 1) * ORI, lanes] = total

    def score_half(h):
        widen(h)

        def some(group, carry):
            steps = [h * 32 + group * 4 + j for j in range(4)]
            add_scores([(m, correlate(m, m)) for m in steps])
            return carry

        lax.fori_loop(0, 8, some, 0)

    for dz in range(4):
        far_x(dz, 0)
    score_half(0)
    add_scores([(FREQ, correlate(FREQ, 0))])
    for dz in range(4):
        far_x(dz, 1)
    score_half(1)

    half_energy = 0.5 * jnp.sum(energy[...], axis=1, keepdims=True)
    peak = jnp.full((ORI, 128), -1e30, F32)
    for b in range(4):
        q1 = acc[b, :ORI, :128] - half_energy
        q2 = acc[b, :ORI, 128:]
        q4 = acc[b, ORI:, :128]
        q3 = acc[b, ORI:, 128:]
        for tau in (1, -1) if b else (1,):
            for sigma in (1, -1):
                entry = entry_of(sigma, tau * b)
                value = q1 - sigma * q3
                if b:
                    value = value - tau * (sigma * q2 + q4)
                expo[entry] = value
                live = counts[entry : entry + 1, :] > 0
                peak = jnp.maximum(peak, jnp.where(live, value, -1e30))
    peak = jnp.max(peak, axis=0, keepdims=True)
    peak = jnp.maximum(peak, pltpu.roll(peak, 32, 1))
    peak = jnp.maximum(peak, pltpu.roll(peak, 64, 1))
    mass = jnp.zeros((ORI, 128), F32)
    for entry in range(14):
        count = counts[entry : entry + 1, :]
        value = jnp.where(count > 0, expo[entry] - peak, -1e30)
        value = jnp.exp(value) * count
        expo[entry] = value
        mass = mass + value
    mass = jnp.sum(mass, axis=0, keepdims=True)
    mass = mass + pltpu.roll(mass, 32, 1)
    mass = mass + pltpu.roll(mass, 64, 1)
    own_peak = peak
    rest = jnp.zeros((6, 128), F32)
    stats_own[...] = jnp.concatenate([peak, mass, rest], axis=0)

    near = [put(stats_own, stats_near.at[s], 41 + s, near_peers[s]) for s in range(3)]
    for b in range(4):
        q1 = jnp.zeros((ORI, 128), F32)
        q2, q3, q4 = q1, q1, q1
        for tau in (1, -1) if b else (1,):
            for sigma in (1, -1):
                value = expo[entry_of(sigma, tau * b)]
                q1 = q1 + value
                q2 = q2 - (sigma * tau) * value
                q3 = q3 - sigma * value
                q4 = q4 - tau * value
        post[b, :ORI, :128] = q1
        post[b, :ORI, 128:] = q2
        post[b, ORI:, :128] = q4
        post[b, ORI:, 128:] = q3

    def spread(first, count):
        def one(m, carry):
            for k in range(2):
                for half in range(2):
                    even = k == half
                    lanes = slice(half * 128, half * 128 + 128)
                    total = None
                    for b in range(4):
                        if b == 0 and not even:
                            continue
                        value = post[b, k * ORI : (k + 1) * ORI, lanes]
                        if b:
                            value = value * sums[m, pl.ds(b if even else 4 + b, 1), :]
                        total = value if total is None else total + value
                    back[m, k * ORI : (k + 1) * ORI, lanes] = total
            return carry

        lax.fori_loop(first, first + count, one, 0)

    for copy in near:
        copy.wait_recv()
    peak, mass = merge_stats([stats_own[...]] + [stats_near[s] for s in range(3)])
    stats_mid[...] = jnp.concatenate([peak, mass, rest], axis=0)
    far = [put(stats_mid, stats_far.at[s], 44 + s, y_peers[s]) for s in range(7)]
    spread(0, STEPS)
    for copy in far:
        copy.wait_recv()
    peak, mass = merge_stats([stats_mid[...]] + [stats_far[s] for s in range(7)])
    loglik = peak + jnp.log(mass)
    loglik_ref[...] = jnp.where(c == 0, loglik[:, :16], loglik[:, 16:32])
    scale = jnp.exp(own_peak - peak) / mass
    scale = jnp.concatenate([scale, scale], axis=1)

    def collect(m):
        grad = jnp.dot((back[m] * scale).astype(BF16), high[m], preferred_element_type=F32)
        out_real = grad[:ORI, :128] + sign * grad[ORI:, 128:]
        out_imag = grad[:ORI, 128:] - sign * grad[ORI:, :128]
        return jnp.concatenate([out_real, out_imag], axis=0)

    def some_back(group, carry):
        for j in range(4):
            m = group * 4 + j
            folded[m] = collect(m)
        return carry

    lax.fori_loop(0, FREQ // 4, some_back, 0)
    folded[0] = folded[0] + collect(FREQ)
    get_kernels.wait()

    def insert(block, first, second):
        value = jnp.where(low, first, second)
        top = value.astype(BF16)
        left = jnp.concatenate([top, (value - top.astype(F32)).astype(BF16)], axis=0)
        out = jnp.dot(left, kernels[block], preferred_element_type=F32)
        out = out[: 2 * ORI] + out[2 * ORI :]
        at = lax.rem(block, 16) * 128 + (block // 16) * ORI
        rows = pl.ds(pl.multiple_of(at, ORI), ORI)
        inserted[rows, :] = jnp.concatenate([out[:ORI], out[ORI:]], axis=1).astype(BF16)

    def some_insert(group, carry):
        for j in range(2):
            b = group * 2 + j
            insert(32 + b, folded[2 * b], pltpu.roll(folded[2 * b + 1], 64, 1))
            m = FREQ - 2 * b
            insert(b, pltpu.roll(folded[lax.rem(m, FREQ)], 64, 1), folded[m - 1])
        return carry

    lax.fori_loop(0, 16, some_insert, 0)

    def scatter(cc):
        def one(t, carry):
            rows = pl.ds(pl.multiple_of(cc * 768 + t * 256, 256), 256)
            part[rows, :] = jnp.dot(
                chosen[rows, :], inserted[...], preferred_element_type=F32
            )
            return carry

        lax.fori_loop(0, 3, one, 0)

    def core_rows(cc):
        return pl.ds(pl.multiple_of(cc * 768, 768), 768)

    scatter(1 - c)
    to_core = put(part.at[core_rows(1 - c)], cores, 51, core_peer)
    scatter(c)
    to_core.wait_recv()

    def chunk(xx):
        return pl.ds(pl.multiple_of(xx * 192, 192), 192)

    def own_chunk(xx):
        return pl.ds(pl.multiple_of(c * 768 + xx * 192, 192), 192)

    steps = []
    for s in (2, 1, 3):
        xx = lax.rem(x + s, 4)
        x_out[s - 1] = (part[own_chunk(xx), :] + cores[chunk(xx), :]).astype(BF16)
        steps.append(put(x_out.at[s - 1], x_in.at[s - 1], 51 + s, x_peers[s - 1]))
    x_own[...] = part[own_chunk(x), :] + cores[chunk(x), :]
    for copy in steps:
        copy.wait_recv()
    x_own[...] += sum(x_in[s].astype(F32) for s in range(3))
    for zz in range(8):
        rows = jnp.concatenate(
            [x_own[k * 64 + zz * 8 : k * 64 + zz * 8 + 8, :] for k in range(3)], axis=1
        )
        rows = jnp.concatenate([rows[:, :384], rows[:, 384:]], axis=0)
        z_own[zz] = rows
        z_out[zz] = rows.astype(BF16)
    steps = [
        put(z_out.at[lax.rem(z + s, 8)], z_in.at[s - 1], 54 + s, z_peers[s - 1])
        for s in range(1, 8)
    ]
    for copy in steps:
        copy.wait_recv()
    total = z_own[z]
    for s in range(7):
        total = total + z_in[s].astype(F32)
    for yy in range(8):
        for j in range(6):
            row = (j // 3) * 8 + yy
            y_out[yy, j : j + 1, :] = total[row : row + 1, (j % 3) * 128 : (j % 3) * 128 + 128]
        y_out[yy, 6:8, :] = jnp.zeros((2, 128), F32)
    steps = [
        put(y_out.at[lax.rem(y + s, 8)], y_in.at[s - 1], 61 + s, y_peers[s - 1])
        for s in range(1, 8)
    ]
    for copy in steps:
        copy.wait_recv()
    total = y_out[y]
    for s in range(7):
        total = total + y_in[s]
    for k in range(3):
        volume_ref[k] = total[2 * k : 2 * k + 2]
    for copy in sends:
        copy.wait_send()


def shards(images, slices, noise_weight, shifts, kernels, targets):
    trig, sums = tables()
    in_vmem = pl.BlockSpec(memory_space=pltpu.VMEM)
    in_smem = pl.BlockSpec(memory_space=pltpu.SMEM)
    anywhere = pl.BlockSpec(memory_space=pl.ANY)
    volume, loglik = pl.pallas_call(
        step_kernel,
        out_shape=(
            jax.ShapeDtypeStruct((3, 2, 128), F32),
            jax.ShapeDtypeStruct((1, 16), F32),
        ),
        in_specs=[
            anywhere, anywhere, in_vmem, in_smem, anywhere, in_vmem, in_vmem, in_vmem,
        ],
        out_specs=(in_vmem, in_vmem),
        scratch_shapes=[
            pltpu.VMEM((16, 2, PIX), BF16),
            pltpu.VMEM((2, 2, PIX), BF16),
            pltpu.VMEM((64, 128, 128), BF16),
            pltpu.VMEM((FREQ, 256), F32),
            pltpu.VMEM((FREQ * 16, 128), F32),
            pltpu.VMEM((FREQ * 16, 128), F32),
            pltpu.VMEM((FREQ, IMGS, 256), BF16),
            pltpu.VMEM((16, 2, FREQ, 256), BF16),
            pltpu.VMEM((72, 128), F32),
            pltpu.VMEM((STEPS, 256, 256), BF16),
            pltpu.VMEM((STEPS, 256, 256), BF16),
            pltpu.VMEM((ORI * FREQ, 128), F32),
            pltpu.VMEM((ORI * FREQ, 128), F32),
            pltpu.VMEM((ORI, 128), F32),
            pltpu.VMEM((4, 2 * ORI, 256), F32),
            pltpu.VMEM((14, ORI, 128), F32),
            pltpu.VMEM((16, 128), F32),
            pltpu.VMEM((16, 128), F32),
            pltpu.VMEM((1536, 2048), BF16),
            pltpu.VMEM((4, 2 * ORI, 256), F32),
            pltpu.VMEM((STEPS, 2 * ORI, 256), F32),
            pltpu.VMEM((FREQ, 2 * ORI, 128), F32),
            pltpu.VMEM((FREQ * ORI, 256), BF16),
            pltpu.VMEM((1536, 256), F32),
            pltpu.VMEM((768, 256), F32),
            pltpu.VMEM((8, 128), F32),
            pltpu.VMEM((3, 8, 128), F32),
            pltpu.VMEM((8, 128), F32),
            pltpu.VMEM((7, 8, 128), F32),
            pltpu.VMEM((3, 192, 256), BF16),
            pltpu.VMEM((3, 192, 256), BF16),
            pltpu.VMEM((192, 256), F32),
            pltpu.VMEM((8, 16, 384), BF16),
            pltpu.VMEM((7, 16, 384), BF16),
            pltpu.VMEM((8, 16, 384), F32),
            pltpu.VMEM((8, 8, 128), F32),
            pltpu.VMEM((7, 8, 128), F32),
            pltpu.SemaphoreType.DMA((69,)),
            pltpu.SemaphoreType.DMA((69,)),
            pltpu.SemaphoreType.DMA((3,)),
        ],
        compiler_params=pltpu.CompilerParams(
            vmem_limit_bytes=VMEM_LIMIT, collective_id=0, has_side_effects=True
        ),
        name="expectation_step",
    )(
        images, slices, noise_weight.reshape(64, 128), shifts, kernels, targets,
        jnp.asarray(trig), jnp.asarray(sums),
    )
    return volume, loglik.reshape(16)


def solution(mesh):
    placed = (
        P("dom", None, None),
        P(("orient", "dom"), None, None),
        P(),
        P(),
        P(),
        P("orient", None),
    )
    return jax.shard_map(
        shards,
        mesh=mesh,
        in_specs=placed,
        out_specs=(P(("dom", "orient"), None, None), P("dom")),
        check_vma=False,
    )
```

time: 635 us -> 82.2 us (0.13)
  waiting for transfers between devices: 356 us -> 0 us
  local copies, waits for them, and re-layouts: 89.1 us -> 3.79 us
  Pallas kernels: 0 us -> 77.6 us
  other arithmetic: 67.1 us -> 0 us
  matrix products: 53.3 us -> 0 us
  blocking collectives: 49.4 us -> 0 us
  between operations: 14.1 us -> 0.64 us
    unnamed x3 -> x0, waiting for transfers between devices: 288 us -> none
    pallas_call x0 -> x1, Pallas kernels: none -> 77.6 us  [shards(): pl.pallas_call(step_kernel, out_shape=(jax.ShapeDtypeStruct((3, 2, 128),...]
    all_gather x1 -> x0, waiting for transfers between devices: 67.2 us -> none  [shards(): piece = lax.all_gather(slices, 'dom', axis=0, tiled=True)]
    dot_general x15 -> x0, matrix products: 53.3 us -> none  [the longest x7 41.1 us: back_group(): lax.dot_general(weights, aligned, (((0,), (0,)), ((), ())), preferred_ele...]
    while x22 -> x0, local copies, waits for them, and re-layouts: 38 us -> none
    another operation x8 -> x0, local copies, waits for them, and re-layouts: 27.5 us -> none  [the longest x7 26.7 us: align_images(): return jnp.stack([out_real, out_imag], axis=2).astype(jnp.bfloat16)]
    pmax x1 -> x0, blocking collectives: 25.6 us -> none  [shards(): peak = lax.pmax(local_peak, 'orient')]
    scatter-add x1 -> x0, other arithmetic: 25.2 us -> none  [shards(): jax.ops.segment_sum(inserted, targets.reshape(-1), num_segments=total_blo...]
  transfers between devices with their start and end apart: 2 -> 0, of which waited for: 2 -> 0; matrix products, arithmetic and copies ran while one was open for 0% -> 0% of each run, Pallas kernels for 0% -> 0%
where the time goes in v2:
time: 82.2 us; the launch traced here: 82 us
  Pallas kernels  77.6 us (94%)
  local copies, waits for them, and re-layouts  3.79 us (5%)
    pallas_call x1, Pallas kernels, shards(): pl.pallas_call(step_kernel, out_shape=(jax.ShapeDtypeStruct((3, 2, 128),...  77.6 us
    unnamed x3, local copies, waits for them, and re-layouts  3.79 us

profile of v2, /device:TPU:1, one launch (start us, length us, event | category | flops | bytes accessed | tf_op | source)
XLA Modules:
  0.0 82.0 jit_solution(2551761985577233855)
XLA Ops:
  0.6 1.4 %copy.10.shifts = s32[49,2]{1,0:T(8,128)} copy(s32[49,2]{0,1:T(2,128)} %param.11) | data formatting | bytes 784 | tf_op args[3]
  2.0 77.6 %expectation_step.1 = (f32[3,2,128]{2,1,0:T(2,128)}, f32[1,16]{1,0:T(1,128)}) custom-call(bf16[16,2,8192]{2,1,0:T(2,128)(2,1)} %images_hbm.1, bf16[2,2,8192]{2,1,0:T(2,128)(2,1)} %slices_hbm.1, f32[64,128]{1,0:T(8,128)} %bitcast.2, s32[49,2]{1,0:T(8,128)} %copy.10.shifts, bf16[64,128,128]{2,1,0:T(8,128)(2,1)} %kernels_hbm.1, s32[64,64]{1,0:T(8,128)} %targets.1, ...), custom_call_target="tpu_custom_call" | custom-call | tf_op jit(solution)/shard_map/expectation_step/pallas_call | solution.py:573
  79.6 1.3 %copy.13 = f32[3,2,128]{2,1,0:T(2,128)} copy(f32[3,2,128]{2,1,0:T(2,128)} %get-tuple-element.8) | data formatting | bytes 6144
  80.8 1.1 %copy.14 = f32[16]{0:T(128)} copy(f32[16]{0:T(128)} %bitcast.3) | data formatting | bytes 128

commit v3 on v2

--- a/solution.py
+++ b/solution.py
@@ -72,10 +72,10 @@
 
 
 def step_kernel(
-    images_hbm, slices_hbm, noise_weight, shifts, kernels_hbm, targets, trig, sums,
+    images_hbm, slices_hbm, noise_weight, shifts, kernels_hbm, targets, trig, sums_hbm, trig_t_hbm,
     volume_ref, loglik_ref,
-    images_raw, slices_raw, kernels,
-    fold_rows, image_real, image_imag, images, slices, weight, high, low_part, real, imag, energy, acc, expo,
+    images_raw, slices_raw, kernels, sums,
+    fold_rows, image_real, image_imag, images, slices, weight, trig_t, high, high_t, low_t, real, imag, energy, acc, expo,
     counts, codes, chosen, post, back, folded, inserted, part, cores,
     stats_own, stats_near, stats_mid, stats_far,
     x_out, x_in, x_own, z_out, z_in, z_own, y_out, y_in,
@@ -112,6 +112,10 @@
     get_images.start()
     get_kernels = pltpu.make_async_copy(kernels_hbm, kernels, local.at[2])
     get_kernels.start()
+    get_sums = pltpu.make_async_copy(sums_hbm, sums, local.at[3])
+    get_sums.start()
+    get_trig_t = pltpu.make_async_copy(trig_t_hbm, trig_t, local.at[4])
+    get_trig_t.start()
 
     sends = []
 
@@ -133,7 +137,6 @@
     low = lax.broadcasted_iota(jnp.int32, (1, 128), 1) < 64
     sign = jnp.where(low, 1.0, -1.0).astype(F32)
 
-    home = x * 4 + zh
     get_slices.wait()
     for j in range(2):
         for m in range(FREQ):
@@ -142,7 +145,7 @@
             )
             fold_rows[m : m + 1, :128] = both[0:1]
             fold_rows[m : m + 1, 128:] = both[1:2]
-        slices[home, j] = fold_rows[...].astype(BF16)
+        slices[0, j] = fold_rows[...].astype(BF16)
 
     def fold_images(first, count):
         def one(i, carry):
@@ -184,7 +187,7 @@
         size = lax.broadcasted_iota(jnp.int32, (16, 128), 1) // IMGS
         total = jnp.zeros((16, 128), F32)
         for t in range(TRANS):
-            shift_x, shift_y = shifts[t, 0], shifts[t, 1]
+            shift_x, shift_y = shifts[0, t], shifts[1, t]
             at = jnp.where(shift_x >= 0, 3, 10) + shift_y
             hit = (row == at) & (size == jnp.abs(shift_x))
             total = total + jnp.where(hit, 1.0, 0.0)
@@ -196,11 +199,13 @@
         k = block - 3 * owner
         core_at, z_hi_at, x_at = (owner >> 4) & 1, (owner >> 5) & 3, owner >> 7
         y_at, z_lo_at = (owner >> 1) & 7, owner & 1
-        code = (core_at * 4 + x_at) * 192 + k * 64 + (z_hi_at * 2 + z_lo_at) * 8 + y_at
-        orient = lax.broadcasted_iota(jnp.int32, (64, ORI), 0)
+        code = (x_at * 2 + core_at) * 192 + k * 64 + (z_hi_at * 2 + z_lo_at) * 8 + y_at
+        row = lax.broadcasted_iota(jnp.int32, (64, ORI), 0)
         mine = lax.broadcasted_iota(jnp.int32, (64, ORI), 1)
-        pick = orient == (mine // 2) * 4 + c * 2 + mine % 2
-        pick = jnp.where(pick, 1.0, 0.0).astype(BF16)
+        x_from = (x + (mine >> 3)) & 3
+        z_from = (zh + (mine >> 1)) & 3
+        source = ((x_from * 4 + z_from) * 2 + c) * 2 + (mine & 1)
+        pick = jnp.where(row == source, 1.0, 0.0).astype(BF16)
         dims = (((0,), (0,)), ((), ()))
         upper, lower = (code >> 5).astype(F32), (code & 31).astype(F32)
         upper = lax.dot_general(upper.astype(BF16), pick, dims, preferred_element_type=F32)
@@ -223,26 +228,45 @@
     def wait_images():
         got(images.at[:, image_half(1 - c)], 0)
 
+    spread_images = jnp.where(
+        lax.broadcasted_iota(jnp.int32, (2 * IMGS, 256), 0) % IMGS
+        == lax.broadcasted_iota(jnp.int32, (2 * IMGS, 256), 1) % IMGS,
+        1.0,
+        0.0,
+    ).astype(BF16)
+
     def align(first, count):
         def one(m, carry):
             factors = trig[...] * weight[pl.ds(m, 1), :]
             rows = aligned_rows(images[lax.rem(m, FREQ)].astype(F32), factors)
             for r, row in enumerate(rows):
-                top = row.astype(BF16)
-                high[m, r * IMGS : (r + 1) * IMGS, :] = top
-                low_part[m, r * IMGS : (r + 1) * IMGS, :] = (row - top.astype(F32)).astype(BF16)
+                high[m, r * IMGS : (r + 1) * IMGS, :] = row.astype(BF16)
             return carry
 
         lax.fori_loop(first, first + count, one, 0)
 
-    def slot(dx, dz):
-        return lax.rem(x + dx, 4) * 4 + lax.rem(zh + dz, 4)
+    def align_turned(first, count):
+        def one(m, carry):
+            w = weight[pl.ds(m, 1), :]
+            pair = images[lax.rem(m, FREQ)].astype(F32) * jnp.concatenate([w, w], axis=1)
+            top = pair.astype(BF16)
+            terms = jnp.concatenate([top, (pair - top.astype(F32)).astype(BF16)], axis=0)
+            turned = lax.dot_general(
+                terms, spread_images, (((0,), (0,)), ((), ())), preferred_element_type=F32
+            )
+            turned = turned * trig_t[...]
+            top = turned.astype(BF16)
+            high_t[m] = top
+            low_t[m] = (turned - top.astype(F32)).astype(BF16)
+            return carry
+
+        lax.fori_loop(first, first + count, one, 0)
 
     def piece(dx, dz, h):
-        return slices.at[slot(dx, dz), :, pl.ds(h * 32, 32)]
+        return slices.at[dx * 4 + dz, :, pl.ds(h * 32, 32)]
 
     def single(dx, dz, h, j):
-        return slices.at[slot(dx, dz), j, pl.ds(h * 32, 32)]
+        return slices.at[dx * 4 + dz, j, pl.ds(h * 32, 32)]
 
     def gsem(kind, h):
         return 1 + kind * 2 + h
@@ -250,23 +274,19 @@
     z_up, z_down, x_up, x_down = z_peers[1], z_peers[5], x_peers[0], x_peers[2]
 
     def along_z(h):
-        here = piece(0, 0, h)
-        put(here, here, gsem(0, h), z_up)
-        put(here, here, gsem(1, h), z_down)
+        put(piece(0, 0, h), piece(0, 3, h), gsem(0, h), z_up)
+        put(piece(0, 0, h), piece(0, 1, h), gsem(1, h), z_down)
 
     def along_x(dz, h):
-        here = piece(0, dz, h)
-        put(here, here, gsem(4 + 4 * dz, h), x_up)
-        put(here, here, gsem(5 + 4 * dz, h), x_down)
+        put(piece(0, dz, h), piece(3, dz, h), gsem(4 + 4 * dz, h), x_up)
+        put(piece(0, dz, h), piece(1, dz, h), gsem(5 + 4 * dz, h), x_down)
 
     def pass_z(h):
         got(piece(0, 3, h), gsem(0, h))
-        half = single(0, 3, h, 0)
-        put(half, half, gsem(2, h), z_up)
+        put(single(0, 3, h, 0), single(0, 2, h, 0), gsem(2, h), z_up)
         along_x(3, h)
         got(piece(0, 1, h), gsem(1, h))
-        half = single(0, 1, h, 1)
-        put(half, half, gsem(3, h), z_down)
+        put(single(0, 1, h, 1), single(0, 2, h, 1), gsem(3, h), z_down)
         along_x(1, h)
 
     def far_z(h):
@@ -276,44 +296,40 @@
 
     def pass_x(dz, h):
         got(piece(3, dz, h), gsem(4 + 4 * dz, h))
-        half = single(3, dz, h, 0)
-        put(half, half, gsem(6 + 4 * dz, h), x_up)
+        put(single(3, dz, h, 0), single(2, dz, h, 0), gsem(6 + 4 * dz, h), x_up)
         got(piece(1, dz, h), gsem(5 + 4 * dz, h))
-        half = single(1, dz, h, 1)
-        put(half, half, gsem(7 + 4 * dz, h), x_down)
+        put(single(1, dz, h, 1), single(2, dz, h, 1), gsem(7 + 4 * dz, h), x_down)
 
     def far_x(dz, h):
         got(single(2, dz, h, 0), gsem(6 + 4 * dz, h))
         got(single(2, dz, h, 1), gsem(7 + 4 * dz, h))
 
-    get_images.wait()
-    fold_images(0, 4)
     pl.semaphore_wait(barrier, len(everyone))
     for h in range(2):
         along_z(h)
         along_x(0, h)
-    fold_images(4, 6)
+    get_images.wait()
+    fold_images(0, 16)
+    send_images()
+    fold_weight()
+    count_cells()
+    pass_z(0)
+    pass_z(1)
     pass_x(0, 0)
     pass_x(0, 1)
-    pass_z(0)
-    pass_z(1)
-    fold_images(10, 6)
-    send_images()
-    pass_x(3, 0)
-    pass_x(1, 0)
+    wait_images()
+    get_trig_t.wait()
+    align_turned(0, 24)
     far_z(0)
-    fold_weight()
-    pass_x(3, 1)
-    pass_x(1, 1)
     far_z(1)
-    wait_images()
-    align(0, 20)
+    for h in range(2):
+        pass_x(3, h)
+        pass_x(1, h)
+    align_turned(24, 24)
     pass_x(2, 0)
     pass_x(2, 1)
-    align(20, 45)
-    count_cells()
-    find_codes()
-    choose(0, 12)
+    align_turned(48, 17)
+    get_sums.wait()
 
     acc[...] = jnp.zeros_like(acc)
     energy[...] = jnp.zeros_like(energy)
@@ -339,10 +355,9 @@
             ],
             axis=0,
         ).astype(BF16)
-        dims = (((1,), (1,)), ((), ()))
-        return lax.dot_general(
-            left, high[m], dims, preferred_element_type=F32
-        ) + lax.dot_general(left, low_part[m], dims, preferred_element_type=F32)
+        return jnp.dot(left, high_t[m], preferred_element_type=F32) + jnp.dot(
+            left, low_t[m], preferred_element_type=F32
+        )
 
     def add_scores(parts):
         for b in range(4):
@@ -364,11 +379,11 @@
         widen(h)
 
         def some(group, carry):
-            steps = [h * 32 + group * 4 + j for j in range(4)]
+            steps = [h * 32 + group * 8 + j for j in range(8)]
             add_scores([(m, correlate(m, m)) for m in steps])
             return carry
 
-        lax.fori_loop(0, 8, some, 0)
+        lax.fori_loop(0, 4, some, 0)
 
     for dz in range(4):
         far_x(dz, 0)
@@ -446,12 +461,15 @@
 
         lax.fori_loop(first, first + count, one, 0)
 
+    spread(0, STEPS)
+    find_codes()
     for copy in near:
         copy.wait_recv()
     peak, mass = merge_stats([stats_own[...]] + [stats_near[s] for s in range(3)])
     stats_mid[...] = jnp.concatenate([peak, mass, rest], axis=0)
     far = [put(stats_mid, stats_far.at[s], 44 + s, y_peers[s]) for s in range(7)]
-    spread(0, STEPS)
+    align(0, STEPS)
+    choose(0, 12)
     for copy in far:
         copy.wait_recv()
     peak, mass = merge_stats([stats_mid[...]] + [stats_far[s] for s in range(7)])
@@ -465,16 +483,6 @@
         out_real = grad[:ORI, :128] + sign * grad[ORI:, 128:]
         out_imag = grad[:ORI, 128:] - sign * grad[ORI:, :128]
         return jnp.concatenate([out_real, out_imag], axis=0)
-
-    def some_back(group, carry):
-        for j in range(4):
-            m = group * 4 + j
-            folded[m] = collect(m)
-        return carry
-
-    lax.fori_loop(0, FREQ // 4, some_back, 0)
-    folded[0] = folded[0] + collect(FREQ)
-    get_kernels.wait()
 
     def insert(block, first, second):
         value = jnp.where(low, first, second)
@@ -486,46 +494,55 @@
         rows = pl.ds(pl.multiple_of(at, ORI), ORI)
         inserted[rows, :] = jnp.concatenate([out[:ORI], out[ORI:]], axis=1).astype(BF16)
 
+    def some_back(group, carry):
+        for j in range(16):
+            m = group * 16 + j
+            folded[m] = collect(m)
+        return carry
+
+    lax.fori_loop(0, FREQ // 16, some_back, 0)
+    folded[0] = folded[0] + collect(FREQ)
+    get_kernels.wait()
+
     def some_insert(group, carry):
-        for j in range(2):
-            b = group * 2 + j
+        for j in range(8):
+            b = group * 8 + j
             insert(32 + b, folded[2 * b], pltpu.roll(folded[2 * b + 1], 64, 1))
             m = FREQ - 2 * b
             insert(b, pltpu.roll(folded[lax.rem(m, FREQ)], 64, 1), folded[m - 1])
         return carry
 
-    lax.fori_loop(0, 16, some_insert, 0)
-
-    def scatter(cc):
-        def one(t, carry):
-            rows = pl.ds(pl.multiple_of(cc * 768 + t * 256, 256), 256)
-            part[rows, :] = jnp.dot(
-                chosen[rows, :], inserted[...], preferred_element_type=F32
-            )
-            return carry
-
-        lax.fori_loop(0, 3, one, 0)
-
-    def core_rows(cc):
-        return pl.ds(pl.multiple_of(cc * 768, 768), 768)
-
-    scatter(1 - c)
-    to_core = put(part.at[core_rows(1 - c)], cores, 51, core_peer)
-    scatter(c)
-    to_core.wait_recv()
-
-    def chunk(xx):
-        return pl.ds(pl.multiple_of(xx * 192, 192), 192)
-
-    def own_chunk(xx):
-        return pl.ds(pl.multiple_of(c * 768 + xx * 192, 192), 192)
+    lax.fori_loop(0, 4, some_insert, 0)
+
+    def part_rows(xx, cc):
+        return pl.ds(pl.multiple_of(xx * 384 + cc * 192, 192), 192)
+
+    to_core = {}
+
+    def scatter(s):
+        xx = lax.rem(x + s, 4)
+        rows = pl.ds(pl.multiple_of(xx * 384, 384), 384)
+        part[rows, :] = jnp.dot(chosen[rows, :], inserted[...], preferred_element_type=F32)
+        to_core[s] = put(part.at[part_rows(xx, 1 - c)], cores.at[s], 51 + s, core_peer)
+
+    def both_cores(s):
+        to_core[s].wait_recv()
+        return part[part_rows(lax.rem(x + s, 4), c), :] + cores[s]
 
     steps = []
-    for s in (2, 1, 3):
-        xx = lax.rem(x + s, 4)
-        x_out[s - 1] = (part[own_chunk(xx), :] + cores[chunk(xx), :]).astype(BF16)
-        steps.append(put(x_out.at[s - 1], x_in.at[s - 1], 51 + s, x_peers[s - 1]))
-    x_own[...] = part[own_chunk(x), :] + cores[chunk(x), :]
+
+    def send_x(s):
+        x_out[s - 1] = both_cores(s).astype(BF16)
+        steps.append(put(x_out.at[s - 1], x_in.at[s - 1], 54 + s, x_peers[s - 1]))
+
+    scatter(2)
+    scatter(1)
+    scatter(3)
+    send_x(2)
+    scatter(0)
+    send_x(1)
+    send_x(3)
+    x_own[...] = both_cores(0)
     for copy in steps:
         copy.wait_recv()
     x_own[...] += sum(x_in[s].astype(F32) for s in range(3))
@@ -537,7 +554,7 @@
         z_own[zz] = rows
         z_out[zz] = rows.astype(BF16)
     steps = [
-        put(z_out.at[lax.rem(z + s, 8)], z_in.at[s - 1], 54 + s, z_peers[s - 1])
+        put(z_out.at[lax.rem(z + s, 8)], z_in.at[s - 1], 57 + s, z_peers[s - 1])
         for s in range(1, 8)
     ]
     for copy in steps:
@@ -551,7 +568,7 @@
             y_out[yy, j : j + 1, :] = total[row : row + 1, (j % 3) * 128 : (j % 3) * 128 + 128]
         y_out[yy, 6:8, :] = jnp.zeros((2, 128), F32)
     steps = [
-        put(y_out.at[lax.rem(y + s, 8)], y_in.at[s - 1], 61 + s, y_peers[s - 1])
+        put(y_out.at[lax.rem(y + s, 8)], y_in.at[s - 1], 64 + s, y_peers[s - 1])
         for s in range(1, 8)
     ]
     for copy in steps:
@@ -565,8 +582,14 @@
         copy.wait_send()
 
 
+def finish_kernel(volume, loglik, volume_ref, loglik_ref):
+    volume_ref[...] = volume[...]
+    loglik_ref[...] = loglik[...]
+
+
 def shards(images, slices, noise_weight, shifts, kernels, targets):
     trig, sums = tables()
+    trig_t = np.repeat(np.concatenate([trig, trig], axis=1).T, IMGS, axis=1)
     in_vmem = pl.BlockSpec(memory_space=pltpu.VMEM)
     in_smem = pl.BlockSpec(memory_space=pltpu.SMEM)
     anywhere = pl.BlockSpec(memory_space=pl.ANY)
@@ -577,19 +600,22 @@
             jax.ShapeDtypeStruct((1, 16), F32),
         ),
         in_specs=[
-            anywhere, anywhere, in_vmem, in_smem, anywhere, in_vmem, in_vmem, in_vmem,
+            anywhere, anywhere, in_vmem, in_smem, anywhere, in_vmem, in_vmem, anywhere, anywhere,
         ],
         out_specs=(in_vmem, in_vmem),
         scratch_shapes=[
             pltpu.VMEM((16, 2, PIX), BF16),
             pltpu.VMEM((2, 2, PIX), BF16),
             pltpu.VMEM((64, 128, 128), BF16),
+            pltpu.VMEM((STEPS, 8, 128), F32),
             pltpu.VMEM((FREQ, 256), F32),
             pltpu.VMEM((FREQ * 16, 128), F32),
             pltpu.VMEM((FREQ * 16, 128), F32),
             pltpu.VMEM((FREQ, IMGS, 256), BF16),
             pltpu.VMEM((16, 2, FREQ, 256), BF16),
             pltpu.VMEM((72, 128), F32),
+            pltpu.VMEM((256, 256), F32),
+            pltpu.VMEM((STEPS, 256, 256), BF16),
             pltpu.VMEM((STEPS, 256, 256), BF16),
             pltpu.VMEM((STEPS, 256, 256), BF16),
             pltpu.VMEM((ORI * FREQ, 128), F32),
@@ -605,7 +631,7 @@
             pltpu.VMEM((FREQ, 2 * ORI, 128), F32),
             pltpu.VMEM((FREQ * ORI, 256), BF16),
             pltpu.VMEM((1536, 256), F32),
-            pltpu.VMEM((768, 256), F32),
+            pltpu.VMEM((4, 192, 256), F32),
             pltpu.VMEM((8, 128), F32),
             pltpu.VMEM((3, 8, 128), F32),
             pltpu.VMEM((8, 128), F32),
@@ -618,18 +644,28 @@
             pltpu.VMEM((8, 16, 384), F32),
             pltpu.VMEM((8, 8, 128), F32),
             pltpu.VMEM((7, 8, 128), F32),
-            pltpu.SemaphoreType.DMA((69,)),
-            pltpu.SemaphoreType.DMA((69,)),
-            pltpu.SemaphoreType.DMA((3,)),
+            pltpu.SemaphoreType.DMA((72,)),
+            pltpu.SemaphoreType.DMA((72,)),
+            pltpu.SemaphoreType.DMA((5,)),
         ],
         compiler_params=pltpu.CompilerParams(
             vmem_limit_bytes=VMEM_LIMIT, collective_id=0, has_side_effects=True
         ),
         name="expectation_step",
     )(
-        images, slices, noise_weight.reshape(64, 128), shifts, kernels, targets,
-        jnp.asarray(trig), jnp.asarray(sums),
+        images, slices, noise_weight.reshape(64, 128), shifts.T, kernels, targets,
+        jnp.asarray(trig), jnp.asarray(sums), jnp.asarray(trig_t),
     )
+    volume, loglik = pl.pallas_call(
+        finish_kernel,
+        out_shape=(
+            jax.ShapeDtypeStruct((3, 2, 128), F32),
+            jax.ShapeDtypeStruct((1, 16), F32),
+        ),
+        in_specs=[in_vmem, in_vmem],
+        out_specs=(in_vmem, in_vmem),
+        name="finish",
+    )(volume, loglik)
     return volume, loglik.reshape(16)
 
 

time: 82.2 us -> 75.7 us (0.921)
  local copies, waits for them, and re-layouts: 3.79 us -> 0 us
  Pallas kernels: 77.6 us -> 74.6 us
    pallas_call x1, Pallas kernels: 77.6 us -> 73.4 us  [shards(): pl.pallas_call(step_kernel, out_shape=(jax.ShapeDtypeStruct((3, 2, 128),...]
    unnamed x3 -> x0, local copies, waits for them, and re-layouts: 3.79 us -> none
    pallas_call x0 -> x1, Pallas kernels: none -> 1.25 us  [shards(): pl.pallas_call(finish_kernel, out_shape=(jax.ShapeDtypeStruct((3, 2, 128)...]
where the time goes in v3:
time: 75.7 us; the launch traced here: 75.3 us
  Pallas kernels  74.6 us (99%)
    pallas_call x1, Pallas kernels, shards(): pl.pallas_call(step_kernel, out_shape=(jax.ShapeDtypeStruct((3, 2, 128),...  73.4 us

profile of v3, /device:TPU:1, one launch (start us, length us, event | category | flops | bytes accessed | tf_op | source)
XLA Modules:
  0.0 75.3 jit_solution(10948771813871493059)
XLA Ops:
  0.6 73.4 %expectation_step.1 = (f32[3,2,128]{2,1,0:T(2,128)}, f32[1,16]{1,0:T(1,128)}) custom-call(bf16[16,2,8192]{2,1,0:T(2,128)(2,1)} %images_hbm.1, bf16[2,2,8192]{2,1,0:T(2,128)(2,1)} %slices_hbm.1, f32[64,128]{1,0:T(8,128)} %bitcast.3, s32[2,49]{1,0:T(2,128)} %bitcast.4, bf16[64,128,128]{2,1,0:T(8,128)(2,1)} %kernels_hbm.1, s32[64,64]{1,0:T(8,128)} %targets.1, ...), custom_call_target="tpu_custom_call" | custom-call | tf_op jit(solution)/shard_map/expectation_step/pallas_call | solution.py:596
  74.0 1.3 %finish.1 = (f32[3,2,128]{2,1,0:T(2,128)}, f32[1,16]{1,0:T(1,128)}) custom-call(f32[3,2,128]{2,1,0:T(2,128)} %get-tuple-element.6.volume, f32[1,16]{1,0:T(1,128)} %get-tuple-element.7.loglik), custom_call_target="tpu_custom_call" | custom-call | tf_op jit(solution)/shard_map/finish/pallas_call | solution.py:659

commit v4 on v3

--- a/solution.py
+++ b/solution.py
@@ -35,6 +35,17 @@
     return rows, sums
 
 
+def repeat(first, count, step, wide=8):
+    def some(group, carry):
+        for j in range(wide):
+            step(first + group * wide + j)
+        return carry
+
+    lax.fori_loop(0, count // wide, some, 0)
+    for j in range(count - count % wide, count):
+        step(first + j)
+
+
 def entry_of(sigma, shift_y):
     return (0 if sigma > 0 else 7) + shift_y + 3
 
@@ -164,13 +175,12 @@
         return pl.ds(pl.multiple_of(cc * 16, 16), 16)
 
     def send_images():
-        def one(m, carry):
+        def one(m):
             at = pl.ds(pl.multiple_of(m * 16, 16), 16)
             rows = jnp.concatenate([image_real[at, :], image_imag[at, :]], axis=1)
             images[m, image_half(c), :] = rows.astype(BF16)
-            return carry
-
-        lax.fori_loop(0, FREQ, one, 0)
+
+        repeat(0, FREQ, one)
         here = images.at[:, image_half(c)]
         put(here, here, 0, core_peer)
 
@@ -236,17 +246,16 @@
     ).astype(BF16)
 
     def align(first, count):
-        def one(m, carry):
+        def one(m):
             factors = trig[...] * weight[pl.ds(m, 1), :]
             rows = aligned_rows(images[lax.rem(m, FREQ)].astype(F32), factors)
             for r, row in enumerate(rows):
                 high[m, r * IMGS : (r + 1) * IMGS, :] = row.astype(BF16)
-            return carry
-
-        lax.fori_loop(first, first + count, one, 0)
+
+        repeat(first, count, one)
 
     def align_turned(first, count):
-        def one(m, carry):
+        def one(m):
             w = weight[pl.ds(m, 1), :]
             pair = images[lax.rem(m, FREQ)].astype(F32) * jnp.concatenate([w, w], axis=1)
             top = pair.astype(BF16)
@@ -258,9 +267,8 @@
             top = turned.astype(BF16)
             high_t[m] = top
             low_t[m] = (turned - top.astype(F32)).astype(BF16)
-            return carry
-
-        lax.fori_loop(first, first + count, one, 0)
+
+        repeat(first, count, one)
 
     def piece(dx, dz, h):
         return slices.at[dx * 4 + dz, :, pl.ds(h * 32, 32)]
@@ -271,38 +279,30 @@
     def gsem(kind, h):
         return 1 + kind * 2 + h
 
-    z_up, z_down, x_up, x_down = z_peers[1], z_peers[5], x_peers[0], x_peers[2]
+    z_up, z_down = z_peers[1], z_peers[5]
 
     def along_z(h):
         put(piece(0, 0, h), piece(0, 3, h), gsem(0, h), z_up)
         put(piece(0, 0, h), piece(0, 1, h), gsem(1, h), z_down)
 
     def along_x(dz, h):
-        put(piece(0, dz, h), piece(3, dz, h), gsem(4 + 4 * dz, h), x_up)
-        put(piece(0, dz, h), piece(1, dz, h), gsem(5 + 4 * dz, h), x_down)
+        for s in range(1, 4):
+            put(piece(0, dz, h), piece(4 - s, dz, h), gsem(3 + 3 * dz + s, h), x_peers[s - 1])
 
     def pass_z(h):
         got(piece(0, 3, h), gsem(0, h))
         put(single(0, 3, h, 0), single(0, 2, h, 0), gsem(2, h), z_up)
-        along_x(3, h)
         got(piece(0, 1, h), gsem(1, h))
         put(single(0, 1, h, 1), single(0, 2, h, 1), gsem(3, h), z_down)
-        along_x(1, h)
 
     def far_z(h):
         got(single(0, 2, h, 0), gsem(2, h))
         got(single(0, 2, h, 1), gsem(3, h))
-        along_x(2, h)
-
-    def pass_x(dz, h):
-        got(piece(3, dz, h), gsem(4 + 4 * dz, h))
-        put(single(3, dz, h, 0), single(2, dz, h, 0), gsem(6 + 4 * dz, h), x_up)
-        got(piece(1, dz, h), gsem(5 + 4 * dz, h))
-        put(single(1, dz, h, 1), single(2, dz, h, 1), gsem(7 + 4 * dz, h), x_down)
-
-    def far_x(dz, h):
-        got(single(2, dz, h, 0), gsem(6 + 4 * dz, h))
-        got(single(2, dz, h, 1), gsem(7 + 4 * dz, h))
+
+    def got_x(h):
+        for dz in (0, 3, 1, 2):
+            for s in range(1, 4):
+                got(piece(4 - s, dz, h), gsem(3 + 3 * dz + s, h))
 
     pl.semaphore_wait(barrier, len(everyone))
     for h in range(2):
@@ -314,35 +314,32 @@
     fold_weight()
     count_cells()
     pass_z(0)
+    along_x(3, 0)
+    along_x(1, 0)
     pass_z(1)
-    pass_x(0, 0)
-    pass_x(0, 1)
+    along_x(3, 1)
     wait_images()
     get_trig_t.wait()
-    align_turned(0, 24)
+    align_turned(0, 16)
     far_z(0)
+    along_x(2, 0)
+    along_x(1, 1)
     far_z(1)
-    for h in range(2):
-        pass_x(3, h)
-        pass_x(1, h)
-    align_turned(24, 24)
-    pass_x(2, 0)
-    pass_x(2, 1)
-    align_turned(48, 17)
+    along_x(2, 1)
+    align_turned(16, STEPS - 16)
     get_sums.wait()
 
     acc[...] = jnp.zeros_like(acc)
     energy[...] = jnp.zeros_like(energy)
 
     def widen(h):
-        def one(o, carry):
+        def one(o):
             block = slices[o // 2, lax.rem(o, 2), pl.ds(h * 32, 32), :].astype(F32)
             rows = pl.ds(pl.multiple_of(o * FREQ + h * 32, 32), 32)
             real[rows, :] = block[:, :128]
             imag[rows, :] = block[:, 128:]
-            return carry
-
-        lax.fori_loop(0, ORI, one, 0)
+
+        repeat(0, ORI, one)
 
     def correlate(m, src):
         at = pl.ds(src, ORI, stride=FREQ)
@@ -385,12 +382,10 @@
 
         lax.fori_loop(0, 4, some, 0)
 
-    for dz in range(4):
-        far_x(dz, 0)
+    got_x(0)
     score_half(0)
     add_scores([(FREQ, correlate(FREQ, 0))])
-    for dz in range(4):
-        far_x(dz, 1)
+    got_x(1)
     score_half(1)
 
     half_energy = 0.5 * jnp.sum(energy[...], axis=1, keepdims=True)
@@ -443,7 +438,7 @@
         post[b, ORI:, 128:] = q3
 
     def spread(first, count):
-        def one(m, carry):
+        def one(m):
             for k in range(2):
                 for half in range(2):
                     even = k == half
@@ -457,9 +452,8 @@
                             value = value * sums[m, pl.ds(b if even else 4 + b, 1), :]
                         total = value if total is None else total + value
                     back[m, k * ORI : (k + 1) * ORI, lanes] = total
-            return carry
-
-        lax.fori_loop(first, first + count, one, 0)
+
+        repeat(first, count, one, 4)
 
     spread(0, STEPS)
     find_codes()

time: 75.7 us -> 67.1 us (0.89)
  Pallas kernels: 74.6 us -> 66 us
    pallas_call x1, Pallas kernels: 73.4 us -> 64.7 us  [shards(): pl.pallas_call(step_kernel, out_shape=(jax.ShapeDtypeStruct((3, 2, 128),...]
where the time goes in v4:
time: 67.1 us; the launch traced here: 66.6 us
  Pallas kernels  66 us (98%)
    pallas_call x1, Pallas kernels, shards(): pl.pallas_call(step_kernel, out_shape=(jax.ShapeDtypeStruct((3, 2, 128),...  64.7 us

profile of v4, /device:TPU:1, one launch (start us, length us, event | category | flops | bytes accessed | tf_op | source)
XLA Modules:
  0.0 66.6 jit_solution(12036966621204632248)
XLA Ops:
  0.6 64.7 %expectation_step.1 = (f32[3,2,128]{2,1,0:T(2,128)}, f32[1,16]{1,0:T(1,128)}) custom-call(bf16[16,2,8192]{2,1,0:T(2,128)(2,1)} %images_hbm.1, bf16[2,2,8192]{2,1,0:T(2,128)(2,1)} %slices_hbm.1, f32[64,128]{1,0:T(8,128)} %bitcast.3, s32[2,49]{1,0:T(2,128)} %bitcast.4, bf16[64,128,128]{2,1,0:T(8,128)(2,1)} %kernels_hbm.1, s32[64,64]{1,0:T(8,128)} %targets.1, ...), custom_call_target="tpu_custom_call" | custom-call | tf_op jit(solution)/shard_map/expectation_step/pallas_call | solution.py:590
  65.3 1.3 %finish.1 = (f32[3,2,128]{2,1,0:T(2,128)}, f32[1,16]{1,0:T(1,128)}) custom-call(f32[3,2,128]{2,1,0:T(2,128)} %get-tuple-element.6.volume, f32[1,16]{1,0:T(1,128)} %get-tuple-element.7.loglik), custom_call_target="tpu_custom_call" | custom-call | tf_op jit(solution)/shard_map/finish/pallas_call | solution.py:653

commit v5 on v4

--- a/solution.py
+++ b/solution.py
@@ -90,7 +90,7 @@
     counts, codes, chosen, post, back, folded, inserted, part, cores,
     stats_own, stats_near, stats_mid, stats_far,
     x_out, x_in, x_own, z_out, z_in, z_own, y_out, y_in,
-    send, recv, local,
+    send, recv, local, heard,
 ):
     dom, ori = lax.axis_index("dom"), lax.axis_index("orient")
     c, zh, x = dom % 2, (dom // 2) % 4, dom // 8
@@ -113,7 +113,8 @@
     y_peers = [dev(0, 0, 0, s) for s in range(1, 8)]
     near_peers = [core_peer, dev_zl(1, 0), dev_zl(1, 1)]
     barrier = pltpu.get_barrier_semaphore()
-    everyone = [core_peer, near_peers[2]] + x_peers + z_peers + y_peers
+    everyone = [core_peer, near_peers[1], z_peers[1], z_peers[5], y_peers[0], y_peers[6]]
+    everyone += x_peers
     for peer in everyone:
         pl.semaphore_signal(barrier, inc=1, device_id=peer, device_id_type=MESH)
 
@@ -127,6 +128,19 @@
     get_sums.start()
     get_trig_t = pltpu.make_async_copy(trig_t_hbm, trig_t, local.at[4])
     get_trig_t.start()
+
+    def hear_of_y():
+        for step in range(3):
+            pl.semaphore_signal(
+                heard.at[step], inc=1, device_id=y_peers[0], device_id_type=MESH
+            )
+            pl.semaphore_signal(
+                heard.at[3 + step], inc=1, device_id=y_peers[6], device_id_type=MESH
+            )
+            yield
+            pl.semaphore_wait(heard.at[step], 1)
+            pl.semaphore_wait(heard.at[3 + step], 1)
+        yield
 
     sends = []
 
@@ -308,6 +322,8 @@
     for h in range(2):
         along_z(h)
         along_x(0, h)
+    news = hear_of_y()
+    next(news)
     get_images.wait()
     fold_images(0, 16)
     send_images()
@@ -318,6 +334,7 @@
     along_x(1, 0)
     pass_z(1)
     along_x(3, 1)
+    next(news)
     wait_images()
     get_trig_t.wait()
     align_turned(0, 16)
@@ -326,7 +343,9 @@
     along_x(1, 1)
     far_z(1)
     along_x(2, 1)
+    next(news)
     align_turned(16, STEPS - 16)
+    next(news)
     get_sums.wait()
 
     acc[...] = jnp.zeros_like(acc)
@@ -641,6 +660,7 @@
             pltpu.SemaphoreType.DMA((72,)),
             pltpu.SemaphoreType.DMA((72,)),
             pltpu.SemaphoreType.DMA((5,)),
+            pltpu.SemaphoreType.REGULAR((6,)),
         ],
         compiler_params=pltpu.CompilerParams(
             vmem_limit_bytes=VMEM_LIMIT, collective_id=0, has_side_effects=True

time: 67.1 us -> 65.5 us (0.976)
  Pallas kernels: 66 us -> 64.2 us
    pallas_call x1, Pallas kernels: 64.7 us -> 62.9 us  [shards(): pl.pallas_call(step_kernel, out_shape=(jax.ShapeDtypeStruct((3, 2, 128),...]
where the time goes in v5:
time: 65.5 us; the launch traced here: 64.8 us
  Pallas kernels  64.2 us (98%)
    pallas_call x1, Pallas kernels, shards(): pl.pallas_call(step_kernel, out_shape=(jax.ShapeDtypeStruct((3, 2, 128),...  62.9 us

profile of v5, /device:TPU:1, one launch (start us, length us, event | category | flops | bytes accessed | tf_op | source)
XLA Modules:
  0.0 64.8 jit_solution(4697006293897314457)
XLA Ops:
  0.6 62.9 %expectation_step.1 = (f32[3,2,128]{2,1,0:T(2,128)}, f32[1,16]{1,0:T(1,128)}) custom-call(bf16[16,2,8192]{2,1,0:T(2,128)(2,1)} %images_hbm.1, bf16[2,2,8192]{2,1,0:T(2,128)(2,1)} %slices_hbm.1, f32[64,128]{1,0:T(8,128)} %bitcast.3, s32[2,49]{1,0:T(2,128)} %bitcast.4, bf16[64,128,128]{2,1,0:T(8,128)(2,1)} %kernels_hbm.1, s32[64,64]{1,0:T(8,128)} %targets.1, ...), custom_call_target="tpu_custom_call" | custom-call | tf_op jit(solution)/shard_map/expectation_step/pallas_call | solution.py:609
  63.5 1.3 %finish.1 = (f32[3,2,128]{2,1,0:T(2,128)}, f32[1,16]{1,0:T(1,128)}) custom-call(f32[3,2,128]{2,1,0:T(2,128)} %get-tuple-element.6.volume, f32[1,16]{1,0:T(1,128)} %get-tuple-element.7.loglik), custom_call_target="tpu_custom_call" | custom-call | tf_op jit(solution)/shard_map/finish/pallas_call | solution.py:673

commit v6 on v5

--- a/solution.py
+++ b/solution.py
@@ -395,11 +395,11 @@
         widen(h)
 
         def some(group, carry):
-            steps = [h * 32 + group * 8 + j for j in range(8)]
+            steps = [h * 32 + group * 16 + j for j in range(16)]
             add_scores([(m, correlate(m, m)) for m in steps])
             return carry
 
-        lax.fori_loop(0, 4, some, 0)
+        lax.fori_loop(0, 2, some, 0)
 
     got_x(0)
     score_half(0)
@@ -532,11 +532,15 @@
 
     to_core = {}
 
-    def scatter(s):
-        xx = lax.rem(x + s, 4)
-        rows = pl.ds(pl.multiple_of(xx * 384, 384), 384)
+    def scatter(s, cc):
+        rows = part_rows(lax.rem(x + s, 4), cc)
         part[rows, :] = jnp.dot(chosen[rows, :], inserted[...], preferred_element_type=F32)
-        to_core[s] = put(part.at[part_rows(xx, 1 - c)], cores.at[s], 51 + s, core_peer)
+
+    def scatter_other(s):
+        scatter(s, 1 - c)
+        to_core[s] = put(
+            part.at[part_rows(lax.rem(x + s, 4), 1 - c)], cores.at[s], 51 + s, core_peer
+        )
 
     def both_cores(s):
         to_core[s].wait_recv()
@@ -548,31 +552,31 @@
         x_out[s - 1] = both_cores(s).astype(BF16)
         steps.append(put(x_out.at[s - 1], x_in.at[s - 1], 54 + s, x_peers[s - 1]))
 
-    scatter(2)
-    scatter(1)
-    scatter(3)
-    send_x(2)
-    scatter(0)
-    send_x(1)
-    send_x(3)
+    for s in (2, 1, 3):
+        scatter_other(s)
+    for s in (2, 1, 3):
+        scatter(s, c)
+        send_x(s)
+    scatter_other(0)
+    scatter(0, c)
     x_own[...] = both_cores(0)
     for copy in steps:
         copy.wait_recv()
     x_own[...] += sum(x_in[s].astype(F32) for s in range(3))
-    for zz in range(8):
+    def z_chunk(zz):
         rows = jnp.concatenate(
-            [x_own[k * 64 + zz * 8 : k * 64 + zz * 8 + 8, :] for k in range(3)], axis=1
+            [x_own[pl.ds(pl.multiple_of(k * 64 + zz * 8, 8), 8), :] for k in range(3)], axis=1
         )
-        rows = jnp.concatenate([rows[:, :384], rows[:, 384:]], axis=0)
-        z_own[zz] = rows
-        z_out[zz] = rows.astype(BF16)
-    steps = [
-        put(z_out.at[lax.rem(z + s, 8)], z_in.at[s - 1], 57 + s, z_peers[s - 1])
-        for s in range(1, 8)
-    ]
+        return jnp.concatenate([rows[:, :384], rows[:, 384:]], axis=0)
+
+    steps = []
+    for s in (4, 3, 5, 2, 6, 1, 7):
+        z_out[s - 1] = z_chunk(lax.rem(z + s, 8)).astype(BF16)
+        steps.append(put(z_out.at[s - 1], z_in.at[s - 1], 57 + s, z_peers[s - 1]))
+    z_own[...] = z_chunk(z)
     for copy in steps:
         copy.wait_recv()
-    total = z_own[z]
+    total = z_own[...]
     for s in range(7):
         total = total + z_in[s].astype(F32)
     for yy in range(8):
@@ -652,9 +656,9 @@
             pltpu.VMEM((3, 192, 256), BF16),
             pltpu.VMEM((3, 192, 256), BF16),
             pltpu.VMEM((192, 256), F32),
-            pltpu.VMEM((8, 16, 384), BF16),
             pltpu.VMEM((7, 16, 384), BF16),
-            pltpu.VMEM((8, 16, 384), F32),
+            pltpu.VMEM((7, 16, 384), BF16),
+            pltpu.VMEM((16, 384), F32),
             pltpu.VMEM((8, 8, 128), F32),
             pltpu.VMEM((7, 8, 128), F32),
             pltpu.SemaphoreType.DMA((72,)),

time: 65.5 us -> 64.5 us (0.985)
  no operation moved by 1% of the time
where the time goes in v6:
time: 64.5 us; the launch traced here: 64.3 us
  Pallas kernels  63.6 us (99%)
    pallas_call x1, Pallas kernels, shards(): pl.pallas_call(step_kernel, out_shape=(jax.ShapeDtypeStruct((3, 2, 128),...  62.4 us

profile of v6, /device:TPU:1, one launch (start us, length us, event | category | flops | bytes accessed | tf_op | source)
XLA Modules:
  0.0 64.3 jit_solution(236678255622693978)
XLA Ops:
  0.6 62.4 %expectation_step.1 = (f32[3,2,128]{2,1,0:T(2,128)}, f32[1,16]{1,0:T(1,128)}) custom-call(bf16[16,2,8192]{2,1,0:T(2,128)(2,1)} %images_hbm.1, bf16[2,2,8192]{2,1,0:T(2,128)(2,1)} %slices_hbm.1, f32[64,128]{1,0:T(8,128)} %bitcast.3, s32[2,49]{1,0:T(2,128)} %bitcast.4, bf16[64,128,128]{2,1,0:T(8,128)(2,1)} %kernels_hbm.1, s32[64,64]{1,0:T(8,128)} %targets.1, ...), custom_call_target="tpu_custom_call" | custom-call | tf_op jit(solution)/shard_map/expectation_step/pallas_call | solution.py:613
  63.0 1.3 %finish.1 = (f32[3,2,128]{2,1,0:T(2,128)}, f32[1,16]{1,0:T(1,128)}) custom-call(f32[3,2,128]{2,1,0:T(2,128)} %get-tuple-element.6.volume, f32[1,16]{1,0:T(1,128)} %get-tuple-element.7.loglik), custom_call_target="tpu_custom_call" | custom-call | tf_op jit(solution)/shard_map/finish/pallas_call | solution.py:677
